TPU v7x, 128 devices: a whole 4x4x4 slice. The times are simulated.
128 devices in a mesh: row: 8 (over z, core), col: 8 (over x_lo, y), rep: 2 (over x_hi).
Axes of the slice: x: 4 (x_hi: 2, x_lo: 2; x = x_hi * 2 + x_lo), y: 4, z: 4, core: 2. Of those that a mesh axis runs over, the one named last changes fastest.
Arguments:
- pair: bfloat16 [1024, 1024, 128], P('row', 'col'), may hold values from -8 to 8
- w_left: bfloat16 [2, 128, 128], P(None, None, 'rep'), may hold values from -1 to 1
- w_left_gate: bfloat16 [2, 128, 128], P(None, None, 'rep'), may hold values from -0.5 to 0.5
- w_right: bfloat16 [2, 128, 128], P(None, None, 'rep'), may hold values from -0.5 to 0.5
- w_right_gate: bfloat16 [2, 128, 128], P(None, None, 'rep'), may hold values from -0.5 to 0.5
- w_gate: bfloat16 [2, 128, 128], replicated, may hold values from -0.5 to 0.5
- w_out: bfloat16 [2, 128, 128], P(None, 'rep'), may hold values from -0.5 to 0.5
- w_trans_in: bfloat16 [128, 1024], replicated, may hold values from -0.5 to 0.5
- w_trans_out: bfloat16 [512, 128], replicated, may hold values from -0.25 to 0.25
Outputs:
- updated: bfloat16 [1024, 1024, 128], P('row', ('col', 'rep'))
All inputs are finite; a program needn't handle non-finite values.
Results may differ from a plain program's by a relative error of at most 0.013.
Values may be sent and summed in bfloat16 or wider, within the bound.
No kernel may reach another device: no remote copies, remote signals or barrier semaphores. Data moves between devices by JAX's collectives and lax.ppermute only.
A program may use at most 192 MiB of HBM per device.

v0:
```python
import jax
import jax.numpy as jnp
from jax import lax
from jax.sharding import PartitionSpec as P

CH = 128


epsilon = 1e-05


def normalize(values, axis):
    mean_value = jnp.mean(values, axis, keepdims=True)
    square_mean = jnp.mean(values * values, axis, keepdims=True)
    return (values - mean_value) * lax.rsqrt(square_mean - mean_value * mean_value + epsilon)


def assemble(received, row_count, col_count, per_device, tile_len):
    grid = received.reshape(row_count, col_count, per_device, tile_len, tile_len)
    return jnp.transpose(grid, (2, 0, 3, 1, 4)).reshape(
        per_device, row_count * tile_len, col_count * tile_len
    )


def disperse(products, row_count, col_count, per_device, tile_len):
    grid = products.reshape(per_device, row_count, tile_len, col_count, tile_len)
    return jnp.transpose(grid, (1, 3, 0, 2, 4))


def contract(left_full, right_full, outgoing):
    if outgoing:
        return jnp.einsum("cik,cjk->cij", left_full, right_full, preferred_element_type=jnp.float32)
    return jnp.einsum("cki,ckj->cij", left_full, right_full, preferred_element_type=jnp.float32)


def product(left_tile, right_tile, outgoing):
    channels, tile_len = (left_tile.shape[0], left_tile.shape[1])
    row_count = lax.axis_size("row")
    col_count = lax.axis_size("col")
    per_device = channels // (row_count * col_count)
    shape_four = (row_count * col_count, per_device, tile_len, tile_len)
    got_left, got_right = (
        lax.all_to_all(
            left_tile.reshape(shape_four), ("row", "col"), split_axis=0, concat_axis=0, tiled=True
        ),
        lax.all_to_all(
            right_tile.reshape(shape_four), ("row", "col"), split_axis=0, concat_axis=0, tiled=True
        ),
    )
    products = contract(
        assemble(got_left, row_count, col_count, per_device, tile_len),
        assemble(got_right, row_count, col_count, per_device, tile_len),
        outgoing,
    )
    outbound = disperse(products, row_count, col_count, per_device, tile_len).reshape(shape_four)
    returned = lax.all_to_all(
        outbound.astype(jnp.bfloat16), ("row", "col"), split_axis=0, concat_axis=0, tiled=True
    ).astype(outbound.dtype)
    return returned.reshape(channels, tile_len, tile_len)


def update(state, layer_index, outgoing, w_left, w_left_gate, w_right, w_right_gate, w_gate, w_out):
    normed = normalize(state, 2).astype(jnp.bfloat16)
    per_rep = w_left.shape[2]
    weights = jnp.concatenate(
        [
            w_left[layer_index],
            w_left_gate[layer_index],
            w_right[layer_index],
            w_right_gate[layer_index],
        ],
        axis=1,
    )
    linear = jnp.einsum("ikd,dc->cik", normed, weights, preferred_element_type=jnp.float32)
    left_tile = (jax.nn.sigmoid(linear[per_rep : 2 * per_rep]) * linear[:per_rep]).astype(
        jnp.bfloat16
    )
    right_tile = (jax.nn.sigmoid(linear[3 * per_rep :]) * linear[2 * per_rep : 3 * per_rep]).astype(
        jnp.bfloat16
    )
    hidden = product(left_tile, right_tile, outgoing)
    gate_values = jax.nn.sigmoid(
        jnp.einsum("ikd,de->ike", normed, w_gate[layer_index], preferred_element_type=jnp.float32)
    )
    sums_first, sums_second = (
        lax.psum(jnp.sum(hidden, 0).astype(jnp.bfloat16), "rep").astype(jnp.float32),
        lax.psum(jnp.sum(hidden * hidden, 0).astype(jnp.bfloat16), "rep").astype(jnp.float32),
    )
    mean_value = sums_first / CH
    variance = sums_second / CH - mean_value * mean_value
    scaled = ((hidden - mean_value) * lax.rsqrt(variance + epsilon)).astype(jnp.bfloat16)
    partial_out = jnp.einsum(
        "cik,cd->ikd", scaled, w_out[layer_index], preferred_element_type=jnp.float32
    )
    projected = lax.psum(partial_out.astype(jnp.bfloat16), "rep").astype(jnp.float32)
    return state + gate_values * projected


def transition(state, w_trans_in, w_trans_out):
    width = w_trans_out.shape[0]
    normed = normalize(state, 2).astype(jnp.bfloat16)
    inner = jnp.einsum("ijd,de->ije", normed, w_trans_in, preferred_element_type=jnp.float32)
    active = (jax.nn.silu(inner[..., :width]) * inner[..., width:]).astype(jnp.bfloat16)
    return (
        state + jnp.einsum("ije,ed->ijd", active, w_trans_out, preferred_element_type=jnp.float32)
    ).astype(jnp.bfloat16)


def on_device(
    pair, w_left, w_left_gate, w_right, w_right_gate, w_gate, w_out, w_trans_in, w_trans_out
):
    state = pair.astype(jnp.float32)
    for layer_index, outgoing in ((0, True), (1, False)):
        state = update(
            state, layer_index, outgoing, w_left, w_left_gate, w_right, w_right_gate, w_gate, w_out
        )
    half_width = state.shape[1] // lax.axis_size("rep")
    column_half = lax.dynamic_slice_in_dim(state, lax.axis_index("rep") * half_width, half_width, 1)
    return transition(column_half, w_trans_in, w_trans_out)


def solution(mesh):
    placed = (
        P("row", "col", None),
        P(None, None, "rep"),
        P(None, None, "rep"),
        P(None, None, "rep"),
        P(None, None, "rep"),
        P(),
        P(None, "rep", None),
        P(),
        P(),
    )
    return jax.shard_map(
        on_device,
        mesh=mesh,
        in_specs=placed,
        out_specs=P("row", ("col", "rep"), None),
        check_vma=False,
    )
```

profile of v0, /device:TPU:1, one launch (start us, length us, event | category | flops | bytes accessed | tf_op | source)
XLA Modules:
  0.0 622.6 jit_solution(17236383973736473681)
XLA Ops:
  6.5 0.0 copy-start
  6.5 0.0 copy-start.9
  6.6 5.8 convert_reduce_fusion
  12.3 0.0 copy-done.6
  12.3 0.0 copy-done.7
  12.4 0.0 copy-done.8
  12.4 0.0 copy-done.9
  12.4 4.7 fusion.32
  17.1 3.3 fusion.42
  20.4 2.7 copy.27
  23.1 11.1 %all-to-all-start.1 = ((bf16[64,1,128,128]{3,2,1,0:T(8,128)(2,1)}), bf16[64,1,128,128]{3,2,1,0:T(8,128)(2,1)}, u32[]{:S(2)}, u32[]{:S(2)}) async-start(bf16[64,1,128,128]{3,2,1,0:T(8,128)(2,1)} %copy.27), calls=%async_computation.1 | async-start | bytes 4194304 | tf_op jit(solution)/shard_map/all_to_all | solution.py:46
  34.2 0.4 all-reduce.13.cloned.1.call-start
  34.6 0.0 copy-done.3
  34.6 2.7 copy.26
  37.3 25.3 %all-to-all-done.1 = bf16[64,1,128,128]{3,2,1,0:T(8,128)(2,1)} async-done(((bf16[64,1,128,128]{3,2,1,0:T(8,128)(2,1)}), bf16[64,1,128,128]{3,2,1,0:T(8,128)(2,1)}, u32[]{:S(2)}, u32[]{:S(2)}) %all-to-all-start.1) | async-done | bytes 2097184 | tf_op jit(solution)/shard_map/all_to_all | solution.py:46
  62.6 33.5 %all_to_all.30 = bf16[64,1,128,128]{3,2,1,0:T(8,128)(2,1)S(1)} all-to-all(bf16[64,1,128,128]{3,2,1,0:T(8,128)(2,1)} %copy.26), channel_id=1, replica_groups=mesh['row'=8,'col'=8,'rep'=2] {'row','col'}, dimensions={0} | all-to-all | bytes 4194304 | tf_op jit(solution)/shard_map/all_to_all | solution.py:43
  96.1 4.2 bitcast_convert_fusion
  100.3 33.2 %all_to_all.31 = bf16[64,1,128,128]{3,2,1,0:T(8,128)(2,1)S(1)} all-to-all(bf16[64,1,128,128]{3,2,1,0:T(8,128)(2,1)S(1)} %bitcast.130), channel_id=1, replica_groups=mesh['row'=8,'col'=8,'rep'=2] {'row','col'}, dimensions={0} | all-to-all | bytes 4194304 | tf_op jit(solution)/shard_map/all_to_all | solution.py:56
  133.5 1.1 fusion.8
  134.6 0.9 reduce_sum.98
  135.5 0.0 all-reduce.13.cloned.1.call-update
  135.5 0.0 all-reduce.7.cloned.1.call-start
  135.6 26.1 %all-reduce.13.cloned.1.call-done = (bf16[128,128]{1,0:T(8,128)(2,1)}, bf16[128,128]{1,0:T(8,128)(2,1)}) async-done(((bf16[128,128]{1,0:T(8,128)(2,1)}, bf16[128,128]{1,0:T(8,128)(2,1)}), (bf16[128,128]{1,0:T(8,128)(2,1)}, bf16[128,128]{1,0:T(8,128)(2,1)})) %all-reduce.13.cloned.1.call-update) | async-done | bytes 65552 | tf_op jit(solution)/shard_map/psum | solution.py:87
  161.6 0.8 convert_multiply_fusion.4
  162.4 0.8 fusion.36
  163.3 0.0 copy-start.10
  163.3 4.5 convolution_convert_fusion.1
  167.8 0.0 all-reduce.7.cloned.1.call-update
  167.9 116.0 %all-reduce.7.cloned.1.call-done = bf16[128,128,128]{2,1,0:T(8,128)(2,1)} async-done(((bf16[128,128,128]{2,1,0:T(8,128)(2,1)}), bf16[128,128,128]{2,1,0:T(8,128)(2,1)}) %all-reduce.7.cloned.1.call-update) | async-done | bytes 4194320 | tf_op jit(solution)/shard_map/psum | solution.py:95
  283.9 13.0 %fusion.73 = (f32[128,128]{1,0:T(8,128)S(1)}, f32[128,128]{1,0:T(8,128)S(1)}, f32[128,128,128]{2,1,0:T(8,128)S(1)}) fusion(bf16[128,128,128]{2,1,0:T(8,128)(2,1)} %all-reduce.7.cloned.1.call-done, bf16[2,128,128]{2,1,0:T(8,128)(2,1)S(1)} %copy-done.10, bf16[128,128,128]{2,1,0:T(8,128)(2,1)} %param.9, f32[128,128]{1,0:T(8,128)S(1)} %get-tuple-element.25, ...), kind=kOutput, calls=%fused_computation.119 | convolution fusion | flops 566198272 | bytes 21266432 | tf_op jit(solution)/shard_map/ikd,de->ike/dot_general | solution.py:83
  296.8 0.0 copy-start.1
  296.9 4.7 fusion.47
  301.6 2.3 fusion.44
  304.0 2.7 copy.33
  306.6 8.3 %all-to-all-start.4 = ((bf16[64,1,128,128]{3,2,1,0:T(8,128)(2,1)}), bf16[64,1,128,128]{3,2,1,0:T(8,128)(2,1)}, u32[]{:S(2)}, u32[]{:S(2)}) async-start(bf16[64,1,128,128]{3,2,1,0:T(8,128)(2,1)} %copy.33), calls=%async_computation.4 | async-start | bytes 4194304 | tf_op jit(solution)/shard_map/all_to_all | solution.py:46
  314.9 2.7 copy.30
  317.6 25.7 %all-to-all-done.4 = bf16[64,1,128,128]{3,2,1,0:T(8,128)(2,1)} async-done(((bf16[64,1,128,128]{3,2,1,0:T(8,128)(2,1)}), bf16[64,1,128,128]{3,2,1,0:T(8,128)(2,1)}, u32[]{:S(2)}, u32[]{:S(2)}) %all-to-all-start.4) | async-done | bytes 2097184 | tf_op jit(solution)/shard_map/all_to_all | solution.py:46
  343.3 5.0 all-to-all-start.3
  348.3 0.0 all-reduce.11.cloned.1.call-start
  348.4 3.0 copy.34
  351.3 2.0 copy.59
  353.3 3.9 copy.35
  357.3 19.5 %all-to-all-done.3 = bf16[64,1,128,128]{3,2,1,0:T(8,128)(2,1)S(1)} async-done(((bf16[64,1,128,128]{3,2,1,0:T(8,128)(2,1)}), bf16[64,1,128,128]{3,2,1,0:T(8,128)(2,1)S(1)}, u32[]{:S(2)}, u32[]{:S(2)}) %all-to-all-start.3) | async-done | bytes 2097184 | tf_op jit(solution)/shard_map/all_to_all | solution.py:43
  376.8 1.4 copy.31
  378.2 0.6 copy.60
  378.8 2.6 copy.32
  381.4 4.6 convolution_convert_fusion.2
  386.0 33.3 %all_to_all.32 = bf16[64,1,128,128]{3,2,1,0:T(8,128)(2,1)S(1)} all-to-all(bf16[64,1,128,128]{3,2,1,0:T(8,128)(2,1)S(1)} %bitcast.132), channel_id=1, replica_groups=mesh['row'=8,'col'=8,'rep'=2] {'row','col'}, dimensions={0} | all-to-all | bytes 4194304 | tf_op jit(solution)/shard_map/all_to_all | solution.py:56
  419.2 1.1 fusion.11
  420.3 0.9 reduce_sum.102
  421.2 0.0 all-reduce.11.cloned.1.call-update
  421.2 0.3 all-reduce.9.cloned.1.call-start
  421.5 25.2 %all-reduce.11.cloned.1.call-done = (bf16[128,128]{1,0:T(8,128)(2,1)}, bf16[128,128]{1,0:T(8,128)(2,1)}) async-done(((bf16[128,128]{1,0:T(8,128)(2,1)}, bf16[128,128]{1,0:T(8,128)(2,1)}), (bf16[128,128]{1,0:T(8,128)(2,1)}, bf16[128,128]{1,0:T(8,128)(2,1)})) %all-reduce.11.cloned.1.call-update) | async-done | bytes 65552 | tf_op jit(solution)/shard_map/psum | solution.py:87
  446.6 0.8 convert_multiply_fusion.3
  447.5 0.8 fusion.35
  448.3 4.5 convolution_convert_fusion
  452.8 0.0 all-reduce.9.cloned.1.call-update
  452.9 9.4 %fusion.48 = f32[128,128,128]{2,1,0:T(8,128)} fusion(f32[128,128,128]{2,1,0:T(8,128)} %copy-done.1, f32[128,128]{1,0:T(8,128)S(1)} %get-tuple-element.23, f32[128,128]{1,0:T(8,128)S(1)} %get-tuple-element.22, bf16[2,128,128]{2,1,0:T(8,128)(2,1)S(1)} %copy-done.10), kind=kOutput, calls=%fused_computation.74 | convolution fusion | flops 543162368 | bytes 16941056 | tf_op jit(solution)/shard_map/ikd,de->ike/dot_general | solution.py:83
  462.3 106.6 %all-reduce.9.cloned.1.call-done = bf16[128,128,128]{2,1,0:T(8,128)(2,1)} async-done(((bf16[128,128,128]{2,1,0:T(8,128)(2,1)}), bf16[128,128,128]{2,1,0:T(8,128)(2,1)}) %all-reduce.9.cloned.1.call-update) | async-done | bytes 4194320 | tf_op jit(solution)/shard_map/psum | solution.py:95
  568.8 6.4 %fusion.74 = (f32[128,64]{1,0:T(8,128)S(1)}, f32[128,64]{1,0:T(8,128)S(1)}, f32[128,64,128]{2,1,0:T(8,128)S(1)}) fusion(bf16[128,128,128]{2,1,0:T(8,128)(2,1)} %all-reduce.9.cloned.1.call-done, s32[]{:T(128)S(6)} %select_n.3, f32[128,128,128]{2,1,0:T(8,128)} %fusion.48, f32[128,128,128]{2,1,0:T(8,128)} %copy-done.1), kind=kLoop, calls=%fused_computation.120 | loop fusion | flops 9420800 | bytes 14745604 | tf_op jit(solution)/shard_map/reduce_sum | solution.py:13
  575.2 3.5 multiply_convert_fusion.1
  578.8 13.2 %fusion.37 = f32[128,64,1024]{2,0,1:T(8,128)} fusion(bf16[128,64,128]{2,1,0:T(8,128)(2,1)S(1)} %multiply_convert_fusion.1, bf16[128,1024]{1,0:T(8,128)(2,1)S(1)} %copy-done), kind=kOutput, calls=%fused_computation.64 | convolution fusion | flops 2147483648 | bytes 35913728 | tf_op jit(solution)/shard_map/ijd,de->ije/dot_general | solution.py:102
  592.0 12.6 %fusion = bf16[128,64,512]{2,0,1:T(8,128)(2,1)S(1)} fusion(f32[128,64,1024]{2,0,1:T(8,128)} %fusion.37), kind=kLoop, calls=%fused_computation.1 | loop fusion | flops 25165824 | bytes 41943040 | tf_op jit(solution)/shard_map/convert_element_type | solution.py:103
  604.6 11.0 %add_convert_fusion = bf16[128,64,128]{2,1,0:T(8,128)(2,1)} fusion(f32[128,64,128]{2,1,0:T(8,128)S(1)} %get-tuple-element.15, bf16[128,64,512]{2,0,1:T(8,128)(2,1)S(1)} %fusion, bf16[512,128]{1,0:T(8,128)(2,1)S(1)} %copy-done.4), kind=kOutput, calls=%fused_computation.54 | convolution fusion | flops 1075838976 | bytes 14811136 | tf_op jit(solution)/shard_map/ije,ed->ijd/dot_general | solution.py:105
  (18 shorter events, 0.1 us)
Async XLA Ops:
  6.5 572.3 %copy-start = (bf16[128,1024]{1,0:T(8,128)(2,1)S(1)}, bf16[128,1024]{1,0:T(8,128)(2,1)}, u32[]{:S(2)}) copy-start(bf16[128,1024]{1,0:T(8,128)(2,1)} %param.16) | copy-start | bytes 786436
  6.5 5.9 copy-start.2
  6.5 5.8 copy-start.6
  6.5 5.8 copy-start.7
  6.5 5.8 copy-start.8
  6.5 5.8 copy-start.9
  20.4 14.2 %copy-start.3 = (bf16[64,1,128,128]{3,0,2,1:T(8,128)(2,1)S(1)}, bf16[64,1,128,128]{3,0,2,1:T(8,128)(2,1)}, u32[]{:S(2)}) copy-start(bf16[64,1,128,128]{3,0,2,1:T(8,128)(2,1)} %get-tuple-element.19) | copy-start | bytes 6291460
  23.1 39.5 %all-to-all-start.1 = ((bf16[64,1,128,128]{3,2,1,0:T(8,128)(2,1)}), bf16[64,1,128,128]{3,2,1,0:T(8,128)(2,1)}, u32[]{:S(2)}, u32[]{:S(2)}) async-start(bf16[64,1,128,128]{3,2,1,0:T(8,128)(2,1)} %copy.27), calls=%async_computation.1 | async-start | bytes 4194304 | tf_op jit(solution)/shard_map/all_to_all | solution.py:46
  34.2 127.4 %all-reduce.13.cloned.1.call-start = ((), (), s32[]{:S(2)}) async-start(), calls=%async_computation.9 | async-start | bytes 131072 | tf_op jit(solution)/shard_map/psum | solution.py:87
  133.5 29.8 %copy-start.5 = (bf16[2,64,128]{2,1,0:T(8,128)(2,1)S(1)}, bf16[2,64,128]{2,1,0:T(8,128)(2,1)}, u32[]{:S(2)}) copy-start(bf16[2,64,128]{2,1,0:T(8,128)(2,1)} %param.15) | copy-start | bytes 98308
  135.5 148.4 %all-reduce.7.cloned.1.call-start = ((), (), s32[]{:S(2)}) async-start(), calls=%async_computation.6 | async-start | bytes 8388608 | tf_op jit(solution)/shard_map/psum | solution.py:95
  163.3 120.6 %copy-start.10 = (bf16[2,128,128]{2,1,0:T(8,128)(2,1)S(1)}, bf16[2,128,128]{2,1,0:T(8,128)(2,1)}, u32[]{:S(2)}) copy-start(bf16[2,128,128]{2,1,0:T(8,128)(2,1)} %param.14) | copy-start | bytes 196612
  296.8 4.8 copy-start.1
  306.6 36.7 %all-to-all-start.4 = ((bf16[64,1,128,128]{3,2,1,0:T(8,128)(2,1)}), bf16[64,1,128,128]{3,2,1,0:T(8,128)(2,1)}, u32[]{:S(2)}, u32[]{:S(2)}) async-start(bf16[64,1,128,128]{3,2,1,0:T(8,128)(2,1)} %copy.33), calls=%async_computation.4 | async-start | bytes 4194304 | tf_op jit(solution)/shard_map/all_to_all | solution.py:46
  343.3 33.5 %all-to-all-start.3 = ((bf16[64,1,128,128]{3,2,1,0:T(8,128)(2,1)}), bf16[64,1,128,128]{3,2,1,0:T(8,128)(2,1)S(1)}, u32[]{:S(2)}, u32[]{:S(2)}) async-start(bf16[64,1,128,128]{3,2,1,0:T(8,128)(2,1)} %copy.30), calls=%async_computation.3 | async-start | bytes 4194304 | tf_op jit(solution)/shard_map/all_to_all | solution.py:43
  348.3 98.3 %all-reduce.11.cloned.1.call-start = ((), (), s32[]{:S(2)}) async-start(), calls=%async_computation.8 | async-start | bytes 131072 | tf_op jit(solution)/shard_map/psum | solution.py:87
  421.2 147.6 %all-reduce.9.cloned.1.call-start = ((), (), s32[]{:S(2)}) async-start(), calls=%async_computation.7 | async-start | bytes 8388608 | tf_op jit(solution)/shard_map/psum | solution.py:95
  592.0 12.6 %copy-start.4 = (bf16[512,128]{1,0:T(8,128)(2,1)S(1)}, bf16[512,128]{1,0:T(8,128)(2,1)}, u32[]{:S(2)}) copy-start(bf16[512,128]{1,0:T(8,128)(2,1)} %param.17) | copy-start | bytes 393220
Sparse Core Ops, SparseCore 0:
  135.6 25.9 all-reduce.12
  168.0 115.8 all-reduce.6
  421.3 25.2 all-reduce.10
  453.0 115.8 all-reduce.8
where the time goes:
time: 632 us; the launch traced here: 623 us
  waiting for transfers between devices  344 us (54%)
  blocking collectives  100 us (16%)
  matrix products  73.9 us (12%)
  other arithmetic  41.1 us (7%)
  starting transfers between devices  25.1 us (4%)
  local copies, waits for them, and re-layouts  24.1 us (4%)
  between operations  13.9 us (2%)
    psum x2, waiting for transfers between devices, update(): lax.psum(partial_out.astype(jnp.bfloat16), 'rep').astype(jnp.float32)  223 us
    all_to_all x2, blocking collectives, product(): lax.all_to_all(outbound.astype(jnp.bfloat16), ('row', 'col'), split_axis=...  66.5 us
    psum x2, waiting for transfers between devices, update(): lax.psum(jnp.sum(hidden * hidden, 0).astype(jnp.bfloat16), 'rep')  51.3 us
    all_to_all x2, waiting for transfers between devices, product(): lax.all_to_all(right_tile.reshape(shape_four), ('row', 'col'), split_axis...  51 us
    all_to_all x1, blocking collectives, product(): lax.all_to_all(left_tile.reshape(shape_four), ('row', 'col'), split_axis=...  33.5 us
    dot_general x2, matrix products, update(): jnp.einsum('ikd,de->ike', normed, w_gate[layer_index], preferred_element_...  22.4 us
    all_to_all x1, waiting for transfers between devices, product(): lax.all_to_all(left_tile.reshape(shape_four), ('row', 'col'), split_axis=...  19.5 us
    all_to_all x2, starting transfers between devices, product(): lax.all_to_all(right_tile.reshape(shape_four), ('row', 'col'), split_axis...  19.4 us
  transfers between devices with their start and end apart: 7, of which 7 were waited for; matrix products, arithmetic and copies ran while one was open for 4% of the time, Pallas kernels for 0%

commit v1 on v0

v1 whole, which is shorter than its diff:
```python
import functools

import jax
import jax.numpy as jnp
from jax import lax
from jax.experimental import pallas as pl
from jax.experimental.pallas import tpu as pltpu
from jax.sharding import PartitionSpec as P

epsilon = 1e-05
BF16, F32 = jnp.bfloat16, jnp.float32
NT = (((1,), (1,)), ((), ()))
ROWS = 16
VMEM_BYTES = 48 * 1024 * 1024


def params():
    return pltpu.CompilerParams(vmem_limit_bytes=VMEM_BYTES)


def cost(flops, nbytes, transcendentals=0):
    return pl.CostEstimate(
        flops=int(flops), bytes_accessed=int(nbytes), transcendentals=int(transcendentals)
    )


def normalize(values):
    mean = jnp.mean(values, 0, keepdims=True)
    square = jnp.mean(values * values, 0, keepdims=True)
    return (values - mean) * lax.rsqrt(square - mean * mean + epsilon)


def identity(n):
    rows = lax.broadcasted_iota(jnp.int32, (n, n), 0)
    cols = lax.broadcasted_iota(jnp.int32, (n, n), 1)
    return jnp.where(rows == cols, 1.0, 0.0).astype(BF16)


def gated(half_linear, half_gate):
    return half_linear + half_linear * jnp.tanh(half_gate)


def dot(a, b):
    return jnp.dot(a, b, preferred_element_type=F32)


def front_kernel(pair_ref, w_ref, out_ref, spread):
    eye = identity(128)
    weights = w_ref[...]
    group = 4
    for first in range(0, ROWS, group):
        x = pair_ref[first : first + group].reshape(group * 128, 128)
        state = lax.dot_general(eye, x, NT, preferred_element_type=F32)
        linear = dot(weights, normalize(state).astype(BF16))
        left = gated(linear[0:64], linear[64:128])
        right = gated(linear[128:192], linear[192:256])
        for side, tile in enumerate((left, right)):
            for row in range(group):
                spread[side, pl.ds(first + row, 64, stride=ROWS), :] = tile[
                    :, row * 128 : (row + 1) * 128
                ]
    for side in range(2):
        out_ref[:, side] = spread[side].reshape(64, ROWS, 128).astype(BF16)


def front(pair, weights):
    return pl.pallas_call(
        front_kernel,
        name="front",
        grid=(128 // ROWS,),
        in_specs=[
            pl.BlockSpec((ROWS, 128, 128), lambda s: (s, 0, 0)),
            pl.BlockSpec((256, 128), lambda s: (0, 0)),
        ],
        out_specs=pl.BlockSpec((64, 2, ROWS, 128), lambda s: (0, 0, s, 0)),
        out_shape=jax.ShapeDtypeStruct((64, 2, 128, 128), BF16),
        scratch_shapes=[pltpu.VMEM((2, 64 * ROWS, 128), F32)],
        compiler_params=params(),
        cost_estimate=cost(16384 * 128 * 384 * 2, 12 << 20, 1 << 21),
    )(pair, weights)


def turn_kernel(rep_ref, pair_ref, w_ref, state_ref, gate_ref, spread):
    eye = identity(128)
    weights = w_ref[...]
    spread[...] = pair_ref[...].astype(F32).reshape(128 * ROWS, 128)
    group = 4
    for first in range(0, ROWS, group):
        x = jnp.concatenate(
            [spread[pl.ds(first + r, 128, stride=ROWS), :] for r in range(group)], 0
        ).astype(BF16)
        state = lax.dot_general(eye, x, NT, preferred_element_type=F32)
        half_gate = dot(weights, normalize(state).astype(BF16))
        where = slice(first * 128, (first + group) * 128)
        state_ref[:, where] = state.astype(BF16)
        gate_ref[:, where] = (0.5 + 0.5 * jnp.tanh(half_gate)).astype(BF16)


def turn(rep, pair, weights):
    steps = 64 // ROWS
    return pl.pallas_call(
        turn_kernel,
        name="turn",
        grid_spec=pltpu.PrefetchScalarGridSpec(
            num_scalar_prefetch=1,
            grid=(steps,),
            in_specs=[
                pl.BlockSpec((128, ROWS, 128), lambda s, rep: (0, rep[0] * steps + s, 0)),
                pl.BlockSpec((128, 128), lambda s, rep: (0, 0)),
            ],
            out_specs=[pl.BlockSpec((128, ROWS * 128), lambda s, rep: (0, s))] * 2,
            scratch_shapes=[pltpu.VMEM((128 * ROWS, 128), F32)],
        ),
        out_shape=[jax.ShapeDtypeStruct((128, 8192), BF16)] * 2,
        compiler_params=params(),
        cost_estimate=cost(8192 * 128 * 256 * 2, 6 << 20, 1 << 20),
    )(rep, pair, weights)


def gate_kernel(state_ref, w_ref, gate_ref):
    half_gate = dot(w_ref[...], normalize(state_ref[...]).astype(BF16))
    gate_ref[...] = (0.5 + 0.5 * jnp.tanh(half_gate)).astype(BF16)


def output_gate(state, weights):
    return pl.pallas_call(
        gate_kernel,
        name="output_gate",
        grid=(8,),
        in_specs=[
            pl.BlockSpec((128, 1024), lambda s: (0, s)),
            pl.BlockSpec((128, 128), lambda s: (0, 0)),
        ],
        out_specs=pl.BlockSpec((128, 1024), lambda s: (0, s)),
        out_shape=jax.ShapeDtypeStruct((128, 8192), BF16),
        compiler_params=params(),
        cost_estimate=cost(8192 * 128 * 128 * 2, 6 << 20, 1 << 20),
    )(state, weights)


def product_kernel(left_ref, right_ref, out_ref, *, by_row):
    if by_row:
        left = jnp.concatenate(
            [jnp.concatenate([left_ref[r, q, 0] for q in range(8)], 1) for r in range(2)], 0
        )
        pieces = [
            jnp.concatenate([right_ref[r, q, 0] for q in range(8)], 1) for r in range(8)
        ]
    else:
        left = jnp.concatenate(
            [
                jnp.concatenate([left_ref[p, r, q, 0] for r in range(8)], 1)
                for q in range(2)
                for p in range(2)
            ],
            0,
        )
        pieces = [
            jnp.concatenate(
                [
                    jnp.concatenate([right_ref[p, r, q, 0] for r in range(8)], 1)
                    for p in range(2)
                ],
                0,
            )
            for q in range(8)
        ]
    for q in range(0, 8, 2):
        right = jnp.concatenate(pieces[q : q + 2], 0)
        hidden = lax.dot_general(right, left, NT, preferred_element_type=F32).astype(BF16)
        for qq in range(2):
            for p in range(2):
                rows = slice(qq * 128 + p * 64, qq * 128 + p * 64 + 64)
                for r in range(2):
                    out_ref[p, r, q + qq] = hidden[rows, r * 128 : (r + 1) * 128]


def product(received, by_row):
    if by_row:
        left_spec = pl.BlockSpec((2, 8, 1, 128, 128), lambda s: (s, 0, 0, 0, 0))
        right_spec = pl.BlockSpec((8, 8, 1, 128, 128), lambda s: (0, 0, 1, 0, 0))
        view = received.reshape(8, 8, 2, 128, 128)
    else:
        left_spec = pl.BlockSpec((2, 8, 2, 1, 64, 128), lambda s: (0, 0, s, 0, 0, 0))
        right_spec = pl.BlockSpec((2, 8, 8, 1, 64, 128), lambda s: (0, 0, 0, 1, 0, 0))
        view = received.reshape(2, 8, 8, 2, 64, 128)
    out = pl.pallas_call(
        functools.partial(product_kernel, by_row=by_row),
        name="product_out" if by_row else "product_in",
        grid=(4,),
        in_specs=[left_spec, right_spec],
        out_specs=pl.BlockSpec((2, 2, 8, 64, 128), lambda s: (0, s, 0, 0, 0)),
        out_shape=jax.ShapeDtypeStruct((2, 8, 8, 64, 128), BF16),
        compiler_params=params(),
        cost_estimate=cost(2 << 30, 6 << 20),
    )(view, view)
    return out.reshape(128, 64, 128)


def scale_hidden(hidden_ref, spread):
    values = hidden_ref[...].astype(F32)
    scaled = normalize(values)
    spread[...] = scaled.reshape(128 * ROWS, 128)


def middle_kernel(
    hidden_ref, state_ref, gate_ref, w_out_ref, w_ref, new_ref, out_ref, spread, sides
):
    scale_hidden(hidden_ref, spread)
    w_out = w_out_ref[...]
    weights = w_ref[...]
    group = 4
    for first in range(0, ROWS, group):
        where = slice(first * 128, (first + group) * 128)
        scaled = jnp.concatenate(
            [spread[pl.ds(first + r, 128, stride=ROWS), :] for r in range(group)], 1
        ).astype(BF16)
        projected = dot(w_out, scaled)
        state = state_ref[:, where].astype(F32) + gate_ref[:, where].astype(F32) * projected
        new_ref[:, where] = state
        linear = dot(weights, normalize(state).astype(BF16))
        for half in range(2):
            at = half * 256
            left = gated(linear[at : at + 64], linear[at + 64 : at + 128])
            right = gated(linear[at + 128 : at + 192], linear[at + 192 : at + 256])
            for side, tile in enumerate((left, right)):
                for row in range(group):
                    sides[
                        side, pl.ds(half * 64 * ROWS + first + row, 64, stride=ROWS), :
                    ] = tile[:, row * 128 : (row + 1) * 128]
    for side in range(2):
        out_ref[:, side] = sides[side].reshape(128, ROWS, 128).astype(BF16)


def middle(hidden, state, gate, w_out, weights):
    wide = pl.BlockSpec((128, ROWS * 128), lambda s: (0, s))
    return pl.pallas_call(
        middle_kernel,
        name="middle",
        grid=(64 // ROWS,),
        in_specs=[
            pl.BlockSpec((128, ROWS, 128), lambda s: (0, s, 0)),
            wide,
            wide,
            pl.BlockSpec((128, 128), lambda s: (0, 0)),
            pl.BlockSpec((512, 128), lambda s: (0, 0)),
        ],
        out_specs=[wide, pl.BlockSpec((128, 2, ROWS, 128), lambda s: (0, 0, s, 0))],
        out_shape=[
            jax.ShapeDtypeStruct((128, 8192), F32),
            jax.ShapeDtypeStruct((128, 2, 64, 128), BF16),
        ],
        scratch_shapes=[
            pltpu.VMEM((128 * ROWS, 128), F32),
            pltpu.VMEM((2, 128 * ROWS, 128), F32),
        ],
        compiler_params=params(),
        cost_estimate=cost(8192 * 128 * 640 * 2, 14 << 20, 1 << 21),
    )(hidden, state, gate, w_out, weights)


def finish_kernel(
    hidden_ref, state_ref, gate_ref, w_out_ref, w_in_ref, w_down_ref, out_ref, spread
):
    scale_hidden(hidden_ref, spread)
    w_out = w_out_ref[...]
    group = 4
    for first in range(0, ROWS, group):
        where = slice(first * 128, (first + group) * 128)
        scaled = jnp.concatenate(
            [spread[pl.ds(first + r, 128, stride=ROWS), :] for r in range(group)], 1
        ).astype(BF16)
        projected = dot(w_out, scaled)
        state = state_ref[:, where] + gate_ref[:, where].astype(F32) * projected
        normed = normalize(state).astype(BF16)
        inner = dot(w_in_ref[...], normed)
        active = (gated(inner[:512], inner[:512]) * inner[512:]).astype(BF16)
        updated = state + dot(w_down_ref[...], active)
        for row in range(group):
            spread[pl.ds(first + row, 128, stride=ROWS), :] = updated[
                :, row * 128 : (row + 1) * 128
            ].T
    out_ref[...] = spread[...].reshape(128, ROWS, 128).astype(BF16)


def finish(hidden, state, gate, w_out, w_in, w_down):
    wide = pl.BlockSpec((128, ROWS * 128), lambda s: (0, s))
    return pl.pallas_call(
        finish_kernel,
        name="finish",
        grid=(64 // ROWS,),
        in_specs=[
            pl.BlockSpec((128, ROWS, 128), lambda s: (0, s, 0)),
            wide,
            wide,
            pl.BlockSpec((128, 128), lambda s: (0, 0)),
            pl.BlockSpec((1024, 128), lambda s: (0, 0)),
            pl.BlockSpec((128, 512), lambda s: (0, 0)),
        ],
        out_specs=pl.BlockSpec((128, ROWS, 128), lambda s: (0, s, 0)),
        out_shape=jax.ShapeDtypeStruct((128, 64, 128), BF16),
        scratch_shapes=[pltpu.VMEM((128 * ROWS, 128), F32)],
        compiler_params=params(),
        cost_estimate=cost(8192 * 128 * 1664 * 2, 10 << 20, 1 << 22),
    )(hidden, state, gate, w_out, w_in, w_down)


def exchange(values, axes):
    return lax.all_to_all(values, axes, split_axis=0, concat_axis=0, tiled=True)


def on_device(
    pair, w_left, w_left_gate, w_right, w_right_gate, w_gate, w_out, w_trans_in, w_trans_out
):
    rep = lax.axis_index("rep").astype(jnp.int32).reshape(1)
    everywhere = ("rep", "row", "col")
    projections = (
        jnp.concatenate([w_left, w_left_gate, w_right, w_right_gate], 2) * 0.5
    ).astype(BF16).transpose(0, 2, 1)
    gates = (w_gate * 0.5).astype(BF16).transpose(0, 2, 1)
    shared = lax.all_gather(
        jnp.concatenate([projections[1], w_out.reshape(128, 128)], 0), "rep", axis=0
    )
    w_second = shared[:, :256].reshape(512, 128)
    w_outs = shared[:, 256:].reshape(2, 2, 64, 128).transpose(1, 3, 0, 2).reshape(2, 128, 128)
    scale = jnp.where(jnp.arange(1024) < 512, 0.5, 1.0).astype(BF16)
    w_in = (w_trans_in * scale).T
    w_down = w_trans_out.T

    sides = front(pair, projections[0])
    received = exchange(sides, ("row", "col"))
    state, gate = turn(rep, pair, gates[0])
    hidden = exchange(product(received, True), everywhere)
    state, sides = middle(hidden, state, gate, w_outs[0], w_second)
    received = exchange(sides, everywhere)
    gate = output_gate(state, gates[1])
    hidden = exchange(product(received, False), everywhere)
    return finish(hidden, state, gate, w_outs[1], w_in, w_down)


def solution(mesh):
    placed = (
        P("row", "col", None),
        P(None, None, "rep"),
        P(None, None, "rep"),
        P(None, None, "rep"),
        P(None, None, "rep"),
        P(),
        P(None, "rep", None),
        P(),
        P(),
    )
    return jax.shard_map(
        on_device,
        mesh=mesh,
        in_specs=placed,
        out_specs=P("row", ("col", "rep"), None),
        check_vma=False,
    )
```

time: 632 us -> 259 us (0.41); the launches traced: 623 us -> 258 us
  waiting for transfers between devices: 344 us -> 22.7 us
  matrix products: 73.9 us -> 0 us
  Pallas kernels: 0 us -> 65 us
  blocking collectives: 100 us -> 149 us
  other arithmetic: 41.1 us -> 1.06 us
  local copies, waits for them, and re-layouts: 24.1 us -> 6.28 us
  between operations: 13.9 us -> 0.2 us
  starting transfers between devices: 25.1 us -> 13 us
    psum x4 -> x0, waiting for transfers between devices: 274 us -> none  [the longest x2 223 us: update(): lax.psum(partial_out.astype(jnp.bfloat16), 'rep').astype(jnp.float32)]
    dot_general x10 -> x0, matrix products: 73.9 us -> none  [the longest x2 22.4 us: update(): jnp.einsum('ikd,de->ike', normed, w_gate[layer_index], preferred_element_...]
    pallas_call x0 -> x7, Pallas kernels: none -> 65 us  [the longest x1 16.4 us: finish(): pl.pallas_call(finish_kernel, name='finish', grid=(64 // ROWS,), in_specs...]
    all_to_all x3 -> x2, waiting for transfers between devices: 70.6 us -> 22.7 us  [exchange(): return lax.all_to_all(values, axes, split_axis=0, concat_axis=0, tiled=True)]
    all_gather x0 -> x1, blocking collectives: none -> 27.5 us  [on_device(): lax.all_gather(jnp.concatenate([projections[1], w_out.reshape(128, 128)],...]
    all_to_all x3 -> x2, blocking collectives: 100 us -> 122 us  [exchange(): return lax.all_to_all(values, axes, split_axis=0, concat_axis=0, tiled=True)]
    convert_element_type x4 -> x1, other arithmetic: 17.8 us -> 0.01 us  [on_device(): scale = jnp.where(jnp.arange(1024) < 512, 0.5, 1.0).astype(BF16)]
    reduce_sum x6 -> x0, other arithmetic: 16 us -> none  [the longest x2 12.1 us: normalize(): mean_value = jnp.mean(values, axis, keepdims=True)]
  transfers between devices with their start and end apart: 7 -> 2, of which waited for: 7 -> 1; matrix products, arithmetic and copies ran while one was open for 4% -> 0% of each run, Pallas kernels for 0% -> 5%
where the time goes in v1:
time: 259 us; the launch traced here: 258 us
  blocking collectives  149 us (58%)
  Pallas kernels  65 us (25%)
  waiting for transfers between devices  22.7 us (9%)
  starting transfers between devices  13 us (5%)
  local copies, waits for them, and re-layouts  6.28 us (2%)
    all_to_all x2, blocking collectives, exchange(): return lax.all_to_all(values, axes, split_axis=0, concat_axis=0, tiled=True)  122 us
    all_gather x1, blocking collectives, on_device(): lax.all_gather(jnp.concatenate([projections[1], w_out.reshape(128, 128)],...  27.5 us
    all_to_all x2, waiting for transfers between devices, exchange(): return lax.all_to_all(values, axes, split_axis=0, concat_axis=0, tiled=True)  22.7 us
    pallas_call x1, Pallas kernels, finish(): pl.pallas_call(finish_kernel, name='finish', grid=(64 // ROWS,), in_specs...  16.4 us
    all_to_all x2, starting transfers between devices, exchange(): return lax.all_to_all(values, axes, split_axis=0, concat_axis=0, tiled=True)  13 us
    pallas_call x1, Pallas kernels, front(): pl.pallas_call(front_kernel, name='front', grid=(128 // ROWS,), in_specs=...  12.8 us
    pallas_call x1, Pallas kernels, middle(): pl.pallas_call(middle_kernel, name='middle', grid=(64 // ROWS,), in_specs...  11.9 us
    pallas_call x2, Pallas kernels, product(): pl.pallas_call(functools.partial(product_kernel, by_row=by_row), name='pr...  11.4 us
  transfers between devices with their start and end apart: 2, of which 1 were waited for; matrix products, arithmetic and copies ran while one was open for 0% of the time, Pallas kernels for 5%

profile of v1, /device:TPU:1, one launch (start us, length us, event | category | flops | bytes accessed | tf_op | source)
XLA Modules:
  0.0 257.5 jit_solution(17449191200469504043)
XLA Ops:
  0.0 0.8 fusion
  0.9 12.8 %front.1 = bf16[64,2,128,128]{3,2,1,0:T(8,128)(2,1)S(1)} custom-call(bf16[128,128,128]{2,1,0:T(8,128)(2,1)} %pair_ref.3, bf16[256,128]{1,0:T(8,128)(2,1)S(1)} %get-tuple-element.14.w_ref), custom_call_target="tpu_custom_call" | custom-call | flops 1610612736 | bytes 12582912 | tf_op jit(solution)/shard_map/front/pallas_call | solution.py:67
  13.7 61.8 %all_to_all.20 = bf16[64,2,128,128]{3,2,1,0:T(8,128)(2,1)} all-to-all(bf16[64,2,128,128]{3,2,1,0:T(8,128)(2,1)S(1)} %front.1), channel_id=1, replica_groups=mesh['row'=8,'col'=8,'rep'=2] {'row','col'}, dimensions={0} | all-to-all | bytes 8388608 | tf_op jit(solution)/shard_map/all_to_all | solution.py:309
  75.5 5.3 %product_out.1 = bf16[2,8,8,64,128]{4,3,2,1,0:T(8,128)(2,1)S(1)} custom-call(bf16[8,8,2,128,128]{4,3,2,1,0:T(8,128)(2,1)} %bitcast.31, bf16[8,8,2,128,128]{4,3,2,1,0:T(8,128)(2,1)} %bitcast.32), custom_call_target="tpu_custom_call" | custom-call | flops 2147483648 | bytes 6291456 | tf_op jit(solution)/shard_map/product_out/pallas_call | solution.py:187
  80.8 0.0 copy-start
  80.8 1.3 copy-done
  82.1 0.0 copy-start.7
  82.1 0.0 copy-start.6
  82.1 5.7 %all-to-all-start.1 = ((bf16[128,64,128]{2,1,0:T(8,128)(2,1)}), bf16[128,64,128]{2,1,0:T(8,128)(2,1)S(1)}, u32[]{:S(2)}, u32[]{:S(2)}) async-start(bf16[128,64,128]{2,1,0:T(8,128)(2,1)} %bitcast.28), calls=%async_computation.1 | async-start | bytes 4194304 | tf_op jit(solution)/shard_map/all_to_all | solution.py:309
  87.8 0.0 copy-done.7
  87.9 27.5 %all-gather = bf16[768,128]{1,0:T(8,128)(2,1)S(1)} all-gather(bf16[384,128]{1,0:T(8,128)(2,1)S(1)} %pad_maximum_fusion), channel_id=2, replica_groups=mesh['row'=8,'col'=8,'rep'=2] {'rep'}, dimensions={0}, use_global_device_ids=true | all-gather | bytes 294912 | tf_op jit(solution)/shard_map/all_gather | solution.py:321
  115.4 0.1 copy.14.w_out_ref
  115.6 0.0 copy-done.6
  115.6 0.1 copy.13
  115.7 6.6 %turn.1 = (bf16[128,8192]{1,0:T(8,128)(2,1)S(1)}, bf16[128,8192]{1,0:T(8,128)(2,1)S(1)}) custom-call(s32[1]{0:T(128)} %bitcast.4.rep_ref, bf16[128,128,128]{2,1,0:T(8,128)(2,1)} %pair_ref.3, bf16[128,128]{1,0:T(8,128)(2,1)S(1)} %get-tuple-element.18.w_ref), custom_call_target="tpu_custom_call" | custom-call | flops 536870912 | bytes 6291456 | tf_op jit(solution)/shard_map/turn/pallas_call | solution.py:101
  122.3 0.0 copy-start.1
  122.3 1.3 copy-done.1
  123.6 0.0 copy-start.3
  123.6 1.4 copy-done.3
  125.0 0.0 all-to-all-done.1.hidden_ref
  125.0 0.0 copy-start.2
  125.0 1.6 copy-done.2
  126.6 11.9 %middle.1 = (f32[128,8192]{1,0:T(8,128)}, bf16[128,2,64,128]{3,2,1,0:T(8,128)(2,1)}) custom-call(bf16[128,64,128]{2,1,0:T(8,128)(2,1)S(1)} %all-to-all-done.1.hidden_ref, bf16[128,8192]{1,0:T(8,128)(2,1)S(1)} %copy-done.2, bf16[128,8192]{1,0:T(8,128)(2,1)} %copy-done.3, bf16[128,128]{1,0:T(8,128)(2,1)S(1)} %copy.14.w_out_ref, bf16[512,128]{1,0:T(8,128)(2,1)S(1)} %bitcast.29), custom_call_target="tpu_custom_call" | custom-call | flops 1342177280 | bytes 14680064 | tf_op jit(solution)/shard_map/middle/pallas_call | solution.py:237
  138.5 59.9 %all_to_all.21 = bf16[128,2,64,128]{3,2,1,0:T(8,128)(2,1)} all-to-all(bf16[128,2,64,128]{3,2,1,0:T(8,128)(2,1)} %get-tuple-element.11), channel_id=1, replica_groups=mesh['row'=8,'col'=8,'rep'=2] {'rep','row','col'}, dimensions={0} | all-to-all | bytes 8388608 | tf_op jit(solution)/shard_map/all_to_all | solution.py:309
  198.4 6.1 %product_in.1 = bf16[2,8,8,64,128]{4,3,2,1,0:T(8,128)(2,1)} custom-call(bf16[2,8,8,2,64,128]{5,4,3,2,1,0:T(8,128)(2,1)} %bitcast.33, bf16[2,8,8,2,64,128]{5,4,3,2,1,0:T(8,128)(2,1)} %bitcast.34), custom_call_target="tpu_custom_call" | custom-call | flops 2147483648 | bytes 6291456 | tf_op jit(solution)/shard_map/product_in/pallas_call | solution.py:187
  204.5 0.0 copy-start.4
  204.5 0.0 copy-start.5
  204.5 7.3 %all-to-all-start.3 = ((bf16[128,64,128]{2,1,0:T(8,128)(2,1)}), bf16[128,64,128]{2,1,0:T(8,128)(2,1)}, u32[]{:S(2)}, u32[]{:S(2)}) async-start(bf16[128,64,128]{2,1,0:T(8,128)(2,1)} %bitcast.15), calls=%async_computation.3 | async-start | bytes 4194304 | tf_op jit(solution)/shard_map/all_to_all | solution.py:309
  211.9 0.1 copy.17.w_out_ref
  212.0 0.0 copy-done.4
  212.0 0.2 copy.15
  212.2 0.0 copy-done.5
  212.2 0.1 copy.16
  212.3 0.2 multiply_bitcast_fusion.w_in_ref
  212.5 5.9 %output_gate.1.gate_ref = bf16[128,8192]{1,0:T(8,128)(2,1)S(1)} custom-call(f32[128,8192]{1,0:T(8,128)} %get-tuple-element.12.state_ref, bf16[128,128]{1,0:T(8,128)(2,1)S(1)} %get-tuple-element.17.w_ref), custom_call_target="tpu_custom_call" | custom-call | flops 268435456 | bytes 6291456 | tf_op jit(solution)/shard_map/output_gate/pallas_call | solution.py:126
  218.4 22.7 %all-to-all-done.3.hidden_ref = bf16[128,64,128]{2,1,0:T(8,128)(2,1)} async-done(((bf16[128,64,128]{2,1,0:T(8,128)(2,1)}), bf16[128,64,128]{2,1,0:T(8,128)(2,1)}, u32[]{:S(2)}, u32[]{:S(2)}) %all-to-all-start.3) | async-done | bytes 2097184 | tf_op jit(solution)/shard_map/all_to_all | solution.py:309
  241.1 16.4 %finish.1 = bf16[128,64,128]{2,1,0:T(8,128)(2,1)} custom-call(bf16[128,64,128]{2,1,0:T(8,128)(2,1)} %all-to-all-done.3.hidden_ref, f32[128,8192]{1,0:T(8,128)} %get-tuple-element.12.state_ref, bf16[128,8192]{1,0:T(8,128)(2,1)S(1)} %output_gate.1.gate_ref, bf16[128,128]{1,0:T(8,128)(2,1)S(1)} %copy.17.w_out_ref, ...), custom_call_target="tpu_custom_call" | custom-call | flops 3489660928 | bytes 10485760 | tf_op jit(solution)/shard_map/finish/pallas_call | solution.py:288
  (8 shorter events, 0.1 us)
Async XLA Ops:
  80.8 1.3 copy-start
  82.1 5.8 %copy-start.7 = (bf16[2,64,128]{2,1,0:T(8,128)(2,1)S(1)}, bf16[2,64,128]{2,1,0:T(8,128)(2,1)}, u32[]{:S(2)}) copy-start(bf16[2,64,128]{2,1,0:T(8,128)(2,1)} %param.15) | copy-start | bytes 98308
  82.1 33.5 %copy-start.6 = (bf16[2,128,128]{2,1,0:T(8,128)(2,1)S(1)}, bf16[2,128,128]{2,1,0:T(8,128)(2,1)}, u32[]{:S(2)}) copy-start(bf16[2,128,128]{2,1,0:T(8,128)(2,1)} %param.14) | copy-start | bytes 196612
  82.1 42.9 %all-to-all-start.1 = ((bf16[128,64,128]{2,1,0:T(8,128)(2,1)}), bf16[128,64,128]{2,1,0:T(8,128)(2,1)S(1)}, u32[]{:S(2)}, u32[]{:S(2)}) async-start(bf16[128,64,128]{2,1,0:T(8,128)(2,1)} %bitcast.28), calls=%async_computation.1 | async-start | bytes 4194304 | tf_op jit(solution)/shard_map/all_to_all | solution.py:309
  122.3 1.3 copy-start.1
  123.6 1.4 copy-start.3
  125.0 1.6 copy-start.2
  204.5 7.4 %copy-start.4 = (bf16[128,1024]{1,0:T(8,128)(2,1)S(1)}, bf16[128,1024]{1,0:T(8,128)(2,1)}, u32[]{:S(2)}) copy-start(bf16[128,1024]{1,0:T(8,128)(2,1)} %param.16) | copy-start | bytes 786436
  204.5 7.6 %copy-start.5 = (bf16[512,128]{1,0:T(8,128)(2,1)S(1)}, bf16[512,128]{1,0:T(8,128)(2,1)}, u32[]{:S(2)}) copy-start(bf16[512,128]{1,0:T(8,128)(2,1)} %param.17) | copy-start | bytes 393220
  204.5 36.5 %all-to-all-start.3 = ((bf16[128,64,128]{2,1,0:T(8,128)(2,1)}), bf16[128,64,128]{2,1,0:T(8,128)(2,1)}, u32[]{:S(2)}, u32[]{:S(2)}) async-start(bf16[128,64,128]{2,1,0:T(8,128)(2,1)} %bitcast.15), calls=%async_computation.3 | async-start | bytes 4194304 | tf_op jit(solution)/shard_map/all_to_all | solution.py:309

commit v2 on v1

v2 whole, which is shorter than its diff:
```python
import functools

import jax
import jax.numpy as jnp
from jax import lax
from jax.experimental import pallas as pl
from jax.experimental.pallas import tpu as pltpu
from jax.sharding import PartitionSpec as P

epsilon = 1e-05
BF16, F32 = jnp.bfloat16, jnp.float32
NT = (((1,), (1,)), ((), ()))
TN = (((0,), (0,)), ((), ()))
ROWS = 16
PITCH = 17
FRONT_ROWS, FRONT_PITCH = 32, 33
VMEM_BYTES = 60 * 1024 * 1024
FINISH_BYTES = 36 * 1024 * 1024


def params(nbytes=VMEM_BYTES):
    return pltpu.CompilerParams(vmem_limit_bytes=nbytes)


def cost(flops, nbytes, transcendentals=0):
    return pl.CostEstimate(
        flops=int(flops), bytes_accessed=int(nbytes), transcendentals=int(transcendentals)
    )


def normalize(values):
    mean = jnp.mean(values, 0, keepdims=True)
    square = jnp.mean(values * values, 0, keepdims=True)
    return (values - mean) * lax.rsqrt(square - mean * mean + epsilon)


def gated(half_linear, half_gate):
    return half_linear + half_linear * jnp.tanh(half_gate)


def dot(a, b):
    return jnp.dot(a, b, preferred_element_type=F32)


def front_kernel(pair_ref, wl_ref, wlg_ref, wr_ref, wrg_ref, out_ref, spread):
    weights = jnp.concatenate([wl_ref[0], wlg_ref[0], wr_ref[0], wrg_ref[0]], 0) * 0.5
    weights = weights.astype(BF16)
    group = 4
    for first in range(0, FRONT_ROWS, group):
        state = jnp.concatenate(
            [pair_ref[first + row].T for row in range(group)], 1
        ).astype(F32)
        linear = dot(weights, normalize(state).astype(BF16))
        left = gated(linear[0:64], linear[64:128])
        right = gated(linear[128:192], linear[192:256])
        for side, tile in enumerate((left, right)):
            for row in range(group):
                spread[side, pl.ds(first + row, 64, stride=FRONT_PITCH), :] = tile[
                    :, row * 128 : (row + 1) * 128
                ]
    for side in range(2):
        for c in range(64):
            at = c * FRONT_PITCH
            out_ref[c, side] = spread[side, at : at + FRONT_ROWS, :].astype(BF16)


def front(pair, weights):
    return pl.pallas_call(
        front_kernel,
        name="front",
        grid=(128 // FRONT_ROWS,),
        in_specs=[pl.BlockSpec((FRONT_ROWS, 128, 128), lambda s: (s, 0, 0))]
        + [pl.BlockSpec((1, 64, 128), lambda s: (0, 0, 0))] * 4,
        out_specs=pl.BlockSpec((64, 2, FRONT_ROWS, 128), lambda s: (0, 0, s, 0)),
        out_shape=jax.ShapeDtypeStruct((64, 2, 128, 128), BF16),
        scratch_shapes=[pltpu.VMEM((2, 64 * FRONT_PITCH, 128), F32)],
        compiler_params=params(),
        cost_estimate=cost(16384 * 128 * 384 * 2, 12 << 20, 1 << 21),
    )(pair, *weights)


def turn_kernel(rep_ref, pair_ref, w_ref, state_ref, gate_ref, spread):
    weights = w_ref[...]
    for i in range(128):
        spread[i * FRONT_PITCH : i * FRONT_PITCH + FRONT_ROWS, :] = pair_ref[i].astype(F32)
    group = 4
    for first in range(0, FRONT_ROWS, group):
        state = jnp.concatenate(
            [spread[pl.ds(first + r, 128, stride=FRONT_PITCH), :].T for r in range(group)], 1
        )
        half_gate = dot(weights, normalize(state).astype(BF16))
        where = slice(first * 128, (first + group) * 128)
        state_ref[:, where] = state.astype(BF16)
        gate_ref[:, where] = (0.5 + 0.5 * jnp.tanh(half_gate)).astype(BF16)


def turn(rep, pair, weights):
    steps = 64 // FRONT_ROWS
    return pl.pallas_call(
        turn_kernel,
        name="turn",
        grid_spec=pltpu.PrefetchScalarGridSpec(
            num_scalar_prefetch=1,
            grid=(steps,),
            in_specs=[
                pl.BlockSpec((128, FRONT_ROWS, 128), lambda s, rep: (0, rep[0] * steps + s, 0)),
                pl.BlockSpec((128, 128), lambda s, rep: (0, 0)),
            ],
            out_specs=[pl.BlockSpec((128, FRONT_ROWS * 128), lambda s, rep: (0, s))] * 2,
            scratch_shapes=[pltpu.VMEM((128 * FRONT_PITCH, 128), F32)],
        ),
        out_shape=[jax.ShapeDtypeStruct((128, 8192), BF16)] * 2,
        compiler_params=params(),
        cost_estimate=cost(8192 * 128 * 256 * 2, 6 << 20, 1 << 20),
    )(rep, pair, weights)


def gate_kernel(state_ref, w_ref, gate_ref):
    half_gate = dot(w_ref[...], normalize(state_ref[...]).astype(BF16))
    gate_ref[...] = (0.5 + 0.5 * jnp.tanh(half_gate)).astype(BF16)


def output_gate(state, weights):
    return pl.pallas_call(
        gate_kernel,
        name="output_gate",
        grid=(8,),
        in_specs=[
            pl.BlockSpec((128, 1024), lambda s: (0, s)),
            pl.BlockSpec((128, 128), lambda s: (0, 0)),
        ],
        out_specs=pl.BlockSpec((128, 1024), lambda s: (0, s)),
        out_shape=jax.ShapeDtypeStruct((128, 8192), BF16),
        compiler_params=params(),
        cost_estimate=cost(8192 * 128 * 128 * 2, 6 << 20, 1 << 20),
    )(state, weights)


def product_kernel(left_ref, *refs, by_row):
    *right_refs, out_ref = refs
    if by_row:
        left = [jnp.concatenate([left_ref[r, q, 0] for q in range(8)], 1) for r in range(4)]
        pieces = [
            jnp.concatenate([right_refs[r // 2][r % 2, q, 0] for q in range(8)], 1)
            for r in range(8)
        ]
    else:
        left = [
            jnp.concatenate([left_ref[p, r, q, 0] for r in range(8)], 1)
            for q in range(4)
            for p in range(2)
        ]
        pieces = [
            jnp.concatenate(
                [
                    jnp.concatenate([right_refs[q // 2][p, r, q % 2, 0] for r in range(8)], 1)
                    for p in range(2)
                ],
                0,
            )
            for q in range(8)
        ]
    left = jnp.concatenate(left, 0)
    for q in range(0, 8, 2):
        right = jnp.concatenate(pieces[q : q + 2], 0)
        hidden = lax.dot_general(right, left, NT, preferred_element_type=F32).astype(BF16)
        for qq in range(2):
            for p in range(2):
                rows = slice(qq * 128 + p * 64, qq * 128 + p * 64 + 64)
                for r in range(4):
                    out_ref[p, r, q + qq] = hidden[rows, r * 128 : (r + 1) * 128]


def product(received, by_row):
    if by_row:
        left_spec = pl.BlockSpec((4, 8, 1, 128, 128), lambda s: (s, 0, 0, 0, 0))
        right_specs = [
            pl.BlockSpec((2, 8, 1, 128, 128), lambda s, i=i: (i, 0, 1, 0, 0)) for i in range(4)
        ]
        view = received.reshape(8, 8, 2, 128, 128)
    else:
        left_spec = pl.BlockSpec((2, 8, 4, 1, 64, 128), lambda s: (0, 0, s, 0, 0, 0))
        right_specs = [
            pl.BlockSpec((2, 8, 2, 1, 64, 128), lambda s, i=i: (0, 0, i, 1, 0, 0))
            for i in range(4)
        ]
        view = received.reshape(2, 8, 8, 2, 64, 128)
    out = pl.pallas_call(
        functools.partial(product_kernel, by_row=by_row),
        name="product_out" if by_row else "product_in",
        grid=(2,),
        in_specs=[left_spec] + right_specs,
        out_specs=pl.BlockSpec((2, 4, 8, 64, 128), lambda s: (0, s, 0, 0, 0)),
        out_shape=jax.ShapeDtypeStruct((2, 8, 8, 64, 128), BF16),
        compiler_params=params(),
        cost_estimate=cost(2 << 30, 6 << 20),
    )(*[view] * 5)
    return out.reshape(128, 64, 128)


def scale_hidden(hidden_ref, spread):
    total = jnp.zeros((ROWS, 128), F32)
    squares = jnp.zeros((ROWS, 128), F32)
    for c in range(128):
        values = hidden_ref[c].astype(F32)
        total += values
        squares += values * values
    mean = total * (1.0 / 128)
    factor = lax.rsqrt(squares * (1.0 / 128) - mean * mean + epsilon)
    for c in range(128):
        spread[c * PITCH : c * PITCH + ROWS, :] = (
            hidden_ref[c].astype(F32) - mean
        ) * factor
    return jnp.concatenate(
        [spread[pl.ds(r, 128, stride=PITCH), :] for r in range(ROWS)], 1
    ).astype(BF16)


def both_halves(rep_ref, mine, other):
    first = rep_ref[0] == 0
    return jnp.concatenate(
        [jnp.where(first, mine, other), jnp.where(first, other, mine)], 0
    )


def middle_kernel(
    rep_ref, hidden_ref, state_ref, gate_ref, mine_ref, other_ref, new_ref, out_ref,
    spread, sides,
):
    w_out = both_halves(rep_ref, mine_ref[256:320], other_ref[256:320])
    weights = both_halves(rep_ref, mine_ref[:256], other_ref[:256])
    scaled = scale_hidden(hidden_ref, spread)
    projected = lax.dot_general(w_out, scaled, TN, preferred_element_type=F32)
    state = state_ref[...].astype(F32) + gate_ref[...].astype(F32) * projected
    new_ref[...] = state
    linear = dot(weights, normalize(state).astype(BF16))
    for half in range(2):
        at = half * 256
        left = gated(linear[at : at + 64], linear[at + 64 : at + 128])
        right = gated(linear[at + 128 : at + 192], linear[at + 192 : at + 256])
        for side, tile in enumerate((left, right)):
            for row in range(ROWS):
                sides[side, pl.ds(half * 64 * PITCH + row, 64, stride=PITCH), :] = tile[
                    :, row * 128 : (row + 1) * 128
                ]
    for side in range(2):
        for c in range(128):
            out_ref[c, side] = sides[side, c * PITCH : c * PITCH + ROWS, :].astype(BF16)


def middle(rep, hidden, state, gate, mine, other):
    wide = pl.BlockSpec((128, ROWS * 128), lambda s, rep: (0, s))
    halves = pl.BlockSpec((384, 128), lambda s, rep: (0, 0))
    return pl.pallas_call(
        middle_kernel,
        name="middle",
        grid_spec=pltpu.PrefetchScalarGridSpec(
            num_scalar_prefetch=1,
            grid=(64 // ROWS,),
            in_specs=[
                pl.BlockSpec((128, ROWS, 128), lambda s, rep: (0, s, 0)),
                wide,
                wide,
                halves,
                halves,
            ],
            out_specs=[wide, pl.BlockSpec((128, 2, ROWS, 128), lambda s, rep: (0, 0, s, 0))],
            scratch_shapes=[
                pltpu.VMEM((128 * PITCH, 128), F32),
                pltpu.VMEM((2, 128 * PITCH, 128), F32),
            ],
        ),
        out_shape=[
            jax.ShapeDtypeStruct((128, 8192), F32),
            jax.ShapeDtypeStruct((128, 2, 64, 128), BF16),
        ],
        compiler_params=params(),
        cost_estimate=cost(8192 * 128 * 640 * 2, 14 << 20, 1 << 21),
    )(rep, hidden, state, gate, mine, other)


def finish_kernel(
    rep_ref, hidden_ref, state_ref, gate_ref, mine_ref, other_ref, w_in_ref, w_down_ref,
    out_ref, spread, state_scr, normed_scr,
):
    w_out = both_halves(rep_ref, mine_ref[320:], other_ref[320:])
    scaled = scale_hidden(hidden_ref, spread)
    projected = lax.dot_general(w_out, scaled, TN, preferred_element_type=F32)
    state = state_ref[...] + gate_ref[...].astype(F32) * projected
    state_scr[...] = state
    normed_scr[...] = normalize(state).astype(BF16)
    group = 8
    for first in range(0, ROWS, group):
        where = slice(first * 128, (first + group) * 128)
        normed = normed_scr[:, where]
        half_gate = dot(w_in_ref[:512], normed)
        linear = dot(w_in_ref[512:], normed)
        active = (gated(half_gate, half_gate) * linear).astype(BF16)
        updated = state_scr[:, where] + dot(w_down_ref[...], active)
        for row in range(group):
            spread[pl.ds(first + row, 128, stride=PITCH), :] = updated[
                :, row * 128 : (row + 1) * 128
            ].T
    for i in range(128):
        out_ref[i] = spread[i * PITCH : i * PITCH + ROWS, :].astype(BF16)


def finish(rep, hidden, state, gate, mine, other, w_in, w_down):
    wide = pl.BlockSpec((128, ROWS * 128), lambda s, rep: (0, s))
    halves = pl.BlockSpec((384, 128), lambda s, rep: (0, 0))
    return pl.pallas_call(
        finish_kernel,
        name="finish",
        grid_spec=pltpu.PrefetchScalarGridSpec(
            num_scalar_prefetch=1,
            grid=(64 // ROWS,),
            in_specs=[
                pl.BlockSpec((128, ROWS, 128), lambda s, rep: (0, s, 0)),
                wide,
                wide,
                halves,
                halves,
                pl.BlockSpec((1024, 128), lambda s, rep: (0, 0)),
                pl.BlockSpec((128, 512), lambda s, rep: (0, 0)),
            ],
            out_specs=pl.BlockSpec((128, ROWS, 128), lambda s, rep: (0, s, 0)),
            scratch_shapes=[
                pltpu.VMEM((128 * PITCH, 128), F32),
                pltpu.VMEM((128, ROWS * 128), F32),
                pltpu.VMEM((128, ROWS * 128), BF16),
            ],
        ),
        out_shape=jax.ShapeDtypeStruct((128, 64, 128), BF16),
        compiler_params=params(FINISH_BYTES),
        cost_estimate=cost(8192 * 128 * 1664 * 2, 10 << 20, 1 << 22),
    )(rep, hidden, state, gate, mine, other, w_in, w_down)


def exchange(values, axes):
    return lax.all_to_all(values, axes, split_axis=0, concat_axis=0, tiled=True)


def on_device(
    pair, w_left, w_left_gate, w_right, w_right_gate, w_gate, w_out, w_trans_in, w_trans_out
):
    rep = lax.axis_index("rep").astype(jnp.int32).reshape(1)
    everywhere = ("rep", "row", "col")
    projections = [
        w.transpose(0, 2, 1) for w in (w_left, w_left_gate, w_right, w_right_gate)
    ]
    sides = front(pair, projections)
    received = exchange(sides, ("row", "col"))

    mine = jnp.concatenate(
        [(w[1] * 0.5).astype(BF16) for w in projections] + [w_out[0], w_out[1]], 0
    )
    other = lax.ppermute(mine, "rep", [(0, 1), (1, 0)])
    gates = (w_gate * 0.5).astype(BF16).transpose(0, 2, 1)
    scale = jnp.where(jnp.arange(1024) < 512, 0.5, 1.0).astype(BF16)
    w_in = (w_trans_in * scale).T
    w_down = w_trans_out.T
    state, gate = turn(rep, pair, gates[0])
    received, state, gate, gates, w_in, w_down, mine, other = lax.optimization_barrier(
        (received, state, gate, gates, w_in, w_down, mine, other)
    )

    hidden = exchange(product(received, True), everywhere)
    state, sides = middle(rep, hidden, state, gate, mine, other)
    received = exchange(sides, everywhere)
    gate = output_gate(state, gates[1])
    received, gate = lax.optimization_barrier((received, gate))
    hidden = exchange(product(received, False), everywhere)
    return finish(rep, hidden, state, gate, mine, other, w_in, w_down)


def solution(mesh):
    placed = (
        P("row", "col", None),
        P(None, None, "rep"),
        P(None, None, "rep"),
        P(None, None, "rep"),
        P(None, None, "rep"),
        P(),
        P(None, "rep", None),
        P(),
        P(),
    )
    return jax.shard_map(
        on_device,
        mesh=mesh,
        in_specs=placed,
        out_specs=P("row", ("col", "rep"), None),
        check_vma=False,
    )
```

time: 259 us -> 234 us (0.903)
  blocking collectives: 149 us -> 71.4 us
  waiting for transfers between devices: 22.7 us -> 89.3 us
  Pallas kernels: 65 us -> 50.3 us
  starting transfers between devices: 13 us -> 20 us
  local copies, waits for them, and re-layouts: 6.28 us -> 1.72 us
    all_to_all x2, blocking collectives: 122 us -> 71.4 us  [exchange(): return lax.all_to_all(values, axes, split_axis=0, concat_axis=0, tiled=True)]
    ppermute x0 -> x1, waiting for transfers between devices: none -> 42.2 us  [on_device(): other = lax.ppermute(mine, 'rep', [(0, 1), (1, 0)])]
    all_gather x1 -> x0, blocking collectives: 27.5 us -> none  [on_device(): lax.all_gather(jnp.concatenate([projections[1], w_out.reshape(128, 128)],...]
    all_to_all x2, waiting for transfers between devices: 22.7 us -> 47.1 us  [exchange(): return lax.all_to_all(values, axes, split_axis=0, concat_axis=0, tiled=True)]
    pallas_call x3, Pallas kernels: 41.2 us -> 27.4 us  [the longest x1 11.1 us: finish(): pl.pallas_call(finish_kernel, name='finish', grid_spec=pltpu.PrefetchScal...]
    unnamed x19 -> x32, local copies, waits for them, and re-layouts: 6.02 us -> 0.47 us
    all_to_all x2, starting transfers between devices: 13 us -> 17.5 us  [exchange(): return lax.all_to_all(values, axes, split_axis=0, concat_axis=0, tiled=True)]
  transfers between devices with their start and end apart: 2 -> 3, of which waited for: 1 -> 3; matrix products, arithmetic and copies ran while one was open for 0% -> 1% of each run, Pallas kernels for 5% -> 5%
where the time goes in v2:
time: 234 us; the launch traced here: 233 us
  waiting for transfers between devices  89.3 us (38%)
  blocking collectives  71.4 us (31%)
  Pallas kernels  50.3 us (21%)
  starting transfers between devices  20 us (9%)
    all_to_all x2, blocking collectives, exchange(): return lax.all_to_all(values, axes, split_axis=0, concat_axis=0, tiled=True)  71.4 us
    all_to_all x2, waiting for transfers between devices, exchange(): return lax.all_to_all(values, axes, split_axis=0, concat_axis=0, tiled=True)  47.1 us
    ppermute x1, waiting for transfers between devices, on_device(): other = lax.ppermute(mine, 'rep', [(0, 1), (1, 0)])  42.2 us
    all_to_all x2, starting transfers between devices, exchange(): return lax.all_to_all(values, axes, split_axis=0, concat_axis=0, tiled=True)  17.5 us
    pallas_call x1, Pallas kernels, finish(): pl.pallas_call(finish_kernel, name='finish', grid_spec=pltpu.PrefetchScal...  11.1 us
    pallas_call x2, Pallas kernels, product(): pl.pallas_call(functools.partial(product_kernel, by_row=by_row), name='pr...  11 us
    pallas_call x1, Pallas kernels, middle(): pl.pallas_call(middle_kernel, name='middle', grid_spec=pltpu.PrefetchScal...  8.86 us
    pallas_call x1, Pallas kernels, front(): pl.pallas_call(front_kernel, name='front', grid=(128 // FRONT_ROWS,), in_...  7.5 us
  transfers between devices with their start and end apart: 3, of which 3 were waited for; matrix products, arithmetic and copies ran while one was open for 1% of the time, Pallas kernels for 5%

profile of v2, /device:TPU:1, one launch (start us, length us, event | category | flops | bytes accessed | tf_op | source)
XLA Modules:
  0.0 233.2 jit_solution(9693797532416452864)
XLA Ops:
  0.0 7.5 %front.1 = bf16[64,2,128,128]{3,2,1,0:T(8,128)(2,1)} custom-call(bf16[128,128,128]{2,1,0:T(8,128)(2,1)} %pair_ref.3, bf16[2,64,128]{2,1,0:T(8,128)(2,1)} %bitcast.41, bf16[2,64,128]{2,1,0:T(8,128)(2,1)} %bitcast.43, bf16[2,64,128]{2,1,0:T(8,128)(2,1)} %bitcast.45, bf16[2,64,128]{2,1,0:T(8,128)(2,1)} %bitcast.47), custom_call_target="tpu_custom_call" | custom-call | flops 1610612736 | bytes 12582912 | tf_op jit(solution)/shard_map/front/pallas_call | solution.py:68
  7.5 0.0 copy-start.8
  7.5 0.0 copy-start.9
  7.5 0.0 copy-start.10
  7.5 0.0 copy-start.11
  7.5 0.0 copy-start.13
  7.5 0.0 copy-start.12
  7.5 0.0 copy-start.6
  7.6 0.0 copy-start.7
  7.6 11.3 %all-to-all-start = ((bf16[64,2,128,128]{3,2,1,0:T(8,128)(2,1)}), bf16[64,2,128,128]{3,2,1,0:T(8,128)(2,1)}, u32[]{:S(2)}, u32[]{:S(2)}) async-start(bf16[64,2,128,128]{3,2,1,0:T(8,128)(2,1)} %front.1), calls=%async_computation | async-start | bytes 8388608 | tf_op jit(solution)/shard_map/all_to_all | solution.py:340
  18.9 0.0 copy-done.8
  18.9 0.0 copy-done.9
  18.9 0.0 copy-done.10
  18.9 0.0 copy-done.11
  19.0 0.0 copy-done.13
  19.0 0.0 copy-start.2
  19.0 2.5 %collective-permute-start = (bf16[384,128]{1,0:T(8,128)(2,1)S(1)}, bf16[384,128]{1,0:T(8,128)(2,1)S(1)}, u32[]{:S(2)}, u32[]{:S(2)}) collective-permute-start(bf16[384,128]{1,0:T(8,128)(2,1)S(1)} %bitcast_dynamic-update-slice_fusion.mine_ref), channel_id=1, source_target_pairs={{0,1},{1,0},{2,3},{3,2},{4,5},{5,4},{6,7},{7,6},{8,9},{9,8},{10,11... | collective-permute-start | bytes 294920 | tf_op jit(solution)/shard_map/ppermute | solution.py:357
  21.5 0.0 copy-done.12
  21.5 0.1 copy.10
  21.7 0.0 copy-done.6
  21.7 0.2 copy.11
  21.9 0.2 multiply_bitcast_fusion.w_in_ref
  22.1 0.6 slice_bitcast_fusion.w_ref
  22.7 0.0 copy-done.7
  22.7 0.1 copy.12
  22.8 4.7 %turn.1 = (bf16[128,8192]{1,0:T(8,128)(2,1)}, bf16[128,8192]{1,0:T(8,128)(2,1)}) custom-call(s32[1]{0:T(128)} %bitcast.rep_ref, bf16[128,128,128]{2,1,0:T(8,128)(2,1)} %pair_ref.3, bf16[128,128]{1,0:T(8,128)(2,1)} %slice_bitcast_fusion.w_ref), custom_call_target="tpu_custom_call" | custom-call | flops 536870912 | bytes 6291456 | tf_op jit(solution)/shard_map/turn/pallas_call | solution.py:99
  27.5 0.0 copy-done.2
  27.5 42.2 %collective-permute-done.other_ref = bf16[384,128]{1,0:T(8,128)(2,1)S(1)} collective-permute-done((bf16[384,128]{1,0:T(8,128)(2,1)S(1)}, bf16[384,128]{1,0:T(8,128)(2,1)S(1)}, u32[]{:S(2)}, u32[]{:S(2)}) %collective-permute-start) | collective-permute-done | bytes 98336 | tf_op jit(solution)/shard_map/ppermute | solution.py:357
  69.7 0.0 copy-start.4
  69.7 3.6 %all-to-all-done = bf16[64,2,128,128]{3,2,1,0:T(8,128)(2,1)} async-done(((bf16[64,2,128,128]{3,2,1,0:T(8,128)(2,1)}), bf16[64,2,128,128]{3,2,1,0:T(8,128)(2,1)}, u32[]{:S(2)}, u32[]{:S(2)}) %all-to-all-start) | async-done | bytes 4194336 | tf_op jit(solution)/shard_map/all_to_all | solution.py:340
  73.3 5.4 %product_out.1 = bf16[2,8,8,64,128]{4,3,2,1,0:T(8,128)(2,1)} custom-call(bf16[8,8,2,128,128]{4,3,2,1,0:T(8,128)(2,1)} %bitcast.15.left_ref.refs_0_.refs_1_.refs_2_.refs_3_, bf16[8,8,2,128,128]{4,3,2,1,0:T(8,128)(2,1)} %bitcast.15.left_ref.refs_0_.refs_1_.refs_2_.refs_3_, bf16[8,8,2,128,128]{4,3,2,1,0:T(8,128)(2,1)} %bitcast.15.left_ref.refs_0_.refs_1_.refs_2_.refs_3_, ...), custom_call_target="tpu_custom_call" | custom-call | flops 2147483648 | bytes 6291456 | tf_op jit(solution)/shard_map/product_out/pallas_call | solution.py:188
  78.7 0.0 copy-done.4
  78.7 35.2 %all_to_all.20.hidden_ref = bf16[128,64,128]{2,1,0:T(8,128)(2,1)} all-to-all(bf16[128,64,128]{2,1,0:T(8,128)(2,1)} %bitcast.39), channel_id=1, replica_groups=mesh['row'=8,'col'=8,'rep'=2] {'rep','row','col'}, dimensions={0} | all-to-all | bytes 4194304 | tf_op jit(solution)/shard_map/all_to_all | solution.py:340
  113.9 8.9 %middle.1 = (f32[128,8192]{1,0:T(8,128)}, bf16[128,2,64,128]{3,2,1,0:T(8,128)(2,1)}) custom-call(s32[1]{0:T(128)} %bitcast.rep_ref, bf16[128,64,128]{2,1,0:T(8,128)(2,1)} %all_to_all.20.hidden_ref, bf16[128,8192]{1,0:T(8,128)(2,1)} %get-tuple-element.22.state_ref, bf16[128,8192]{1,0:T(8,128)(2,1)} %get-tuple-element.23.gate_ref, bf16[384,128]{1,0:T(8,128)(2,1)} %copy-done.2, ...), custom_call_target="tpu_custom_call" | custom-call | flops 1342177280 | bytes 14680064 | tf_op jit(solution)/shard_map/middle/pallas_call | solution.py:254
  122.7 6.2 %all-to-all-start.2 = ((bf16[128,2,64,128]{3,2,1,0:T(8,128)(2,1)}), bf16[128,2,64,128]{3,2,1,0:T(8,128)(2,1)}, u32[]{:S(2)}, u32[]{:S(2)}) async-start(bf16[128,2,64,128]{3,2,1,0:T(8,128)(2,1)} %get-tuple-element.26), calls=%async_computation.2 | async-start | bytes 8388608 | tf_op jit(solution)/shard_map/all_to_all | solution.py:340
  128.9 0.6 slice_bitcast_fusion.1.w_ref
  129.5 7.2 %output_gate.1.gate_ref = bf16[128,8192]{1,0:T(8,128)(2,1)} custom-call(f32[128,8192]{1,0:T(8,128)} %get-tuple-element.27.state_ref, bf16[128,128]{1,0:T(8,128)(2,1)} %slice_bitcast_fusion.1.w_ref), custom_call_target="tpu_custom_call" | custom-call | flops 268435456 | bytes 6291456 | tf_op jit(solution)/shard_map/output_gate/pallas_call | solution.py:124
  136.7 43.6 %all-to-all-done.2 = bf16[128,2,64,128]{3,2,1,0:T(8,128)(2,1)} async-done(((bf16[128,2,64,128]{3,2,1,0:T(8,128)(2,1)}), bf16[128,2,64,128]{3,2,1,0:T(8,128)(2,1)}, u32[]{:S(2)}, u32[]{:S(2)}) %all-to-all-start.2) | async-done | bytes 4194336 | tf_op jit(solution)/shard_map/all_to_all | solution.py:340
  180.3 0.0 copy-start.1
  180.3 0.0 copy-start.3
  180.3 0.0 copy-start.5
  180.3 5.6 %product_in.1 = bf16[2,8,8,64,128]{4,3,2,1,0:T(8,128)(2,1)} custom-call(bf16[2,8,8,2,64,128]{5,4,3,2,1,0:T(8,128)(2,1)} %bitcast.18.left_ref.refs_0_.refs_1_.refs_2_.refs_3_, bf16[2,8,8,2,64,128]{5,4,3,2,1,0:T(8,128)(2,1)} %bitcast.18.left_ref.refs_0_.refs_1_.refs_2_.refs_3_, ...), custom_call_target="tpu_custom_call" | custom-call | flops 2147483648 | bytes 6291456 | tf_op jit(solution)/shard_map/product_in/pallas_call | solution.py:188
  185.9 0.0 copy-start
  185.9 36.3 %all_to_all.21.hidden_ref = bf16[128,64,128]{2,1,0:T(8,128)(2,1)S(1)} all-to-all(bf16[128,64,128]{2,1,0:T(8,128)(2,1)} %bitcast.40), channel_id=1, replica_groups=mesh['row'=8,'col'=8,'rep'=2] {'rep','row','col'}, dimensions={0} | all-to-all | bytes 4194304 | tf_op jit(solution)/shard_map/all_to_all | solution.py:340
  222.2 0.0 copy-done.1
  222.2 0.0 copy-done.3
  222.2 0.0 copy-done.5
  222.2 0.0 copy-done
  222.2 11.1 %finish.1 = bf16[128,64,128]{2,1,0:T(8,128)(2,1)} custom-call(s32[1]{0:T(128)} %bitcast.rep_ref, bf16[128,64,128]{2,1,0:T(8,128)(2,1)S(1)} %all_to_all.21.hidden_ref, f32[128,8192]{1,0:T(8,128)S(1)} %copy-done, bf16[128,8192]{1,0:T(8,128)(2,1)S(1)} %copy-done.1, bf16[384,128]{1,0:T(8,128)(2,1)S(1)} %copy-done.3, bf16[384,128]{1,0:T(8,128)(2,1)S(1)} %copy-done.5, ...), custom_call_target="tpu_custom_call" | custom-call | flops 3489660928 | bytes 10485760 | tf_op jit(solution)/shard_map/finish/pallas_call | solution.py:311
  (8 shorter events, 0.1 us)
Async XLA Ops:
  7.5 11.4 %copy-start.8 = (bf16[2,128,64]{1,2,0:T(8,128)(2,1)S(1)}, bf16[2,128,64]{1,2,0:T(8,128)(2,1)}, u32[]{:S(2)}) copy-start(bf16[2,128,64]{1,2,0:T(8,128)(2,1)} %param.10) | copy-start | bytes 98308
  7.5 11.4 %copy-start.9 = (bf16[2,128,64]{1,2,0:T(8,128)(2,1)S(1)}, bf16[2,128,64]{1,2,0:T(8,128)(2,1)}, u32[]{:S(2)}) copy-start(bf16[2,128,64]{1,2,0:T(8,128)(2,1)} %param.11) | copy-start | bytes 98308
  7.5 11.4 %copy-start.10 = (bf16[2,128,64]{1,2,0:T(8,128)(2,1)S(1)}, bf16[2,128,64]{1,2,0:T(8,128)(2,1)}, u32[]{:S(2)}) copy-start(bf16[2,128,64]{1,2,0:T(8,128)(2,1)} %param.12) | copy-start | bytes 98308
  7.5 11.4 %copy-start.11 = (bf16[2,128,64]{1,2,0:T(8,128)(2,1)S(1)}, bf16[2,128,64]{1,2,0:T(8,128)(2,1)}, u32[]{:S(2)}) copy-start(bf16[2,128,64]{1,2,0:T(8,128)(2,1)} %param.13) | copy-start | bytes 98308
  7.5 11.4 %copy-start.13 = (bf16[2,64,128]{2,1,0:T(8,128)(2,1)S(1)}, bf16[2,64,128]{2,1,0:T(8,128)(2,1)}, u32[]{:S(2)}) copy-start(bf16[2,64,128]{2,1,0:T(8,128)(2,1)} %param.15) | copy-start | bytes 98308
  7.5 14.0 %copy-start.12 = (bf16[2,128,128]{2,1,0:T(8,128)(2,1)S(1)}, bf16[2,128,128]{2,1,0:T(8,128)(2,1)}, u32[]{:S(2)}) copy-start(bf16[2,128,128]{2,1,0:T(8,128)(2,1)} %param.14) | copy-start | bytes 196612
  7.5 14.1 %copy-start.6 = (bf16[128,1024]{1,0:T(8,128)(2,1)S(1)}, bf16[128,1024]{1,0:T(8,128)(2,1)}, u32[]{:S(2)}) copy-start(bf16[128,1024]{1,0:T(8,128)(2,1)} %param.16) | copy-start | bytes 786436
  7.6 15.1 %copy-start.7 = (bf16[512,128]{1,0:T(8,128)(2,1)S(1)}, bf16[512,128]{1,0:T(8,128)(2,1)}, u32[]{:S(2)}) copy-start(bf16[512,128]{1,0:T(8,128)(2,1)} %param.17) | copy-start | bytes 393220
  7.6 65.7 %all-to-all-start = ((bf16[64,2,128,128]{3,2,1,0:T(8,128)(2,1)}), bf16[64,2,128,128]{3,2,1,0:T(8,128)(2,1)}, u32[]{:S(2)}, u32[]{:S(2)}) async-start(bf16[64,2,128,128]{3,2,1,0:T(8,128)(2,1)} %front.1), calls=%async_computation | async-start | bytes 8388608 | tf_op jit(solution)/shard_map/all_to_all | solution.py:340
  19.0 8.5 %copy-start.2 = (bf16[384,128]{1,0:T(8,128)(2,1)}, bf16[384,128]{1,0:T(8,128)(2,1)S(1)}, u32[]{:S(2)}) copy-start(bf16[384,128]{1,0:T(8,128)(2,1)S(1)} %bitcast_dynamic-update-slice_fusion.mine_ref) | copy-start | bytes 294916
  19.0 50.7 %collective-permute-start = (bf16[384,128]{1,0:T(8,128)(2,1)S(1)}, bf16[384,128]{1,0:T(8,128)(2,1)S(1)}, u32[]{:S(2)}, u32[]{:S(2)}) collective-permute-start(bf16[384,128]{1,0:T(8,128)(2,1)S(1)} %bitcast_dynamic-update-slice_fusion.mine_ref), channel_id=1, source_target_pairs={{0,1},{1,0},{2,3},{3,2},{4,5},{5,4},{6,7},{7,6},{8,9},{9,8},{10,11... | collective-permute-start | bytes 294920 | tf_op jit(solution)/shard_map/ppermute | solution.py:357
  69.7 9.0 %copy-start.4 = (bf16[384,128]{1,0:T(8,128)(2,1)}, bf16[384,128]{1,0:T(8,128)(2,1)S(1)}, u32[]{:S(2)}) copy-start(bf16[384,128]{1,0:T(8,128)(2,1)S(1)} %collective-permute-done.other_ref) | copy-start | bytes 294916
  122.7 57.5 %all-to-all-start.2 = ((bf16[128,2,64,128]{3,2,1,0:T(8,128)(2,1)}), bf16[128,2,64,128]{3,2,1,0:T(8,128)(2,1)}, u32[]{:S(2)}, u32[]{:S(2)}) async-start(bf16[128,2,64,128]{3,2,1,0:T(8,128)(2,1)} %get-tuple-element.26), calls=%async_computation.2 | async-start | bytes 8388608 | tf_op jit(solution)/shard_map/all_to_all | solution.py:340
  180.3 41.9 %copy-start.1 = (bf16[128,8192]{1,0:T(8,128)(2,1)S(1)}, bf16[128,8192]{1,0:T(8,128)(2,1)}, u32[]{:S(2)}) copy-start(bf16[128,8192]{1,0:T(8,128)(2,1)} %output_gate.1.gate_ref) | copy-start | bytes 6291460
  180.3 41.9 %copy-start.3 = (bf16[384,128]{1,0:T(8,128)(2,1)S(1)}, bf16[384,128]{1,0:T(8,128)(2,1)}, u32[]{:S(2)}) copy-start(bf16[384,128]{1,0:T(8,128)(2,1)} %copy-done.2) | copy-start | bytes 294916
  180.3 41.9 %copy-start.5 = (bf16[384,128]{1,0:T(8,128)(2,1)S(1)}, bf16[384,128]{1,0:T(8,128)(2,1)}, u32[]{:S(2)}) copy-start(bf16[384,128]{1,0:T(8,128)(2,1)} %copy-done.4) | copy-start | bytes 294916
  185.9 36.3 %copy-start = (f32[128,8192]{1,0:T(8,128)S(1)}, f32[128,8192]{1,0:T(8,128)}, u32[]{:S(2)}) copy-start(f32[128,8192]{1,0:T(8,128)} %get-tuple-element.27.state_ref) | copy-start | bytes 12582916

commit v3 on v2

v3 whole, which is shorter than its diff:
```python
import functools

import jax
import jax.numpy as jnp
from jax import lax
from jax.experimental import pallas as pl
from jax.experimental.pallas import tpu as pltpu
from jax.sharding import PartitionSpec as P

epsilon = 1e-05
BF16, F32 = jnp.bfloat16, jnp.float32
VMEM = pl.BlockSpec(memory_space=pltpu.VMEM)
SMEM = pl.BlockSpec(memory_space=pltpu.SMEM)
ANY = pl.BlockSpec(memory_space=pl.ANY)
NT = (((1,), (1,)), ((), ()))
TN = (((0,), (0,)), ((), ()))
ROWS = 16
PITCH = 17
FRONT_ROWS, FRONT_PITCH = 32, 33


PRODUCT_MIB, MIDDLE_MIB, FINISH_MIB = 24, 36, 36


def params(mebibytes):
    return pltpu.CompilerParams(vmem_limit_bytes=mebibytes * 1024 * 1024)


def cost(flops, nbytes, transcendentals=0):
    return pl.CostEstimate(
        flops=int(flops), bytes_accessed=int(nbytes), transcendentals=int(transcendentals)
    )


def normalize(values):
    mean = jnp.mean(values, 0, keepdims=True)
    square = jnp.mean(values * values, 0, keepdims=True)
    return (values - mean) * lax.rsqrt(square - mean * mean + epsilon)


def gated(half_linear, half_gate):
    return half_linear + half_linear * jnp.tanh(half_gate)


def dot(a, b):
    return jnp.dot(a, b, preferred_element_type=F32)


def front_kernel(pair_ref, wl_ref, wlg_ref, wr_ref, wrg_ref, out_ref, spread):
    weights = jnp.concatenate([wl_ref[0], wlg_ref[0], wr_ref[0], wrg_ref[0]], 0) * 0.5
    weights = weights.astype(BF16)
    group = 4
    for first in range(0, FRONT_ROWS, group):
        state = jnp.concatenate(
            [pair_ref[first + row].T for row in range(group)], 1
        ).astype(F32)
        linear = dot(weights, normalize(state).astype(BF16))
        left = gated(linear[0:64], linear[64:128])
        right = gated(linear[128:192], linear[192:256])
        for side, tile in enumerate((left, right)):
            for row in range(group):
                spread[side, pl.ds(first + row, 64, stride=FRONT_PITCH), :] = tile[
                    :, row * 128 : (row + 1) * 128
                ]
    for side in range(2):
        for c in range(64):
            at = c * FRONT_PITCH
            out_ref[c, side] = spread[side, at : at + FRONT_ROWS, :].astype(BF16)


def front(pair, weights):
    return pl.pallas_call(
        front_kernel,
        name="front",
        grid=(128 // FRONT_ROWS,),
        in_specs=[pl.BlockSpec((FRONT_ROWS, 128, 128), lambda s: (s, 0, 0))]
        + [pl.BlockSpec((1, 64, 128), lambda s: (0, 0, 0))] * 4,
        out_specs=pl.BlockSpec((64, 2, FRONT_ROWS, 128), lambda s: (0, 0, s, 0)),
        out_shape=pltpu.HBM((64, 2, 128, 128), BF16),
        scratch_shapes=[pltpu.VMEM((2, 64 * FRONT_PITCH, 128), F32)],
        compiler_params=params(60),
        cost_estimate=cost(16384 * 128 * 384 * 2, 12 << 20, 1 << 21),
    )(pair, *weights)


def turn_kernel(rep_ref, pair_ref, w_ref, state_ref, gate_ref, spread):
    weights = w_ref[...]
    for i in range(128):
        spread[i * FRONT_PITCH : i * FRONT_PITCH + FRONT_ROWS, :] = pair_ref[i].astype(F32)
    group = 4
    for first in range(0, FRONT_ROWS, group):
        state = jnp.concatenate(
            [spread[pl.ds(first + r, 128, stride=FRONT_PITCH), :].T for r in range(group)], 1
        )
        half_gate = dot(weights, normalize(state).astype(BF16))
        where = slice(first * 128, (first + group) * 128)
        state_ref[:, where] = state.astype(BF16)
        gate_ref[:, where] = (0.5 + 0.5 * jnp.tanh(half_gate)).astype(BF16)


def turn(rep, pair, weights):
    steps = 64 // FRONT_ROWS
    return pl.pallas_call(
        turn_kernel,
        name="turn",
        grid_spec=pltpu.PrefetchScalarGridSpec(
            num_scalar_prefetch=1,
            grid=(steps,),
            in_specs=[
                pl.BlockSpec((128, FRONT_ROWS, 128), lambda s, rep: (0, rep[0] * steps + s, 0)),
                pl.BlockSpec((128, 128), lambda s, rep: (0, 0)),
            ],
            out_specs=[pl.BlockSpec((128, FRONT_ROWS * 128), lambda s, rep: (0, s))] * 2,
            scratch_shapes=[pltpu.VMEM((128 * FRONT_PITCH, 128), F32)],
        ),
        out_shape=[pltpu.HBM((128, 8192), BF16)] * 2,
        compiler_params=params(36),
        cost_estimate=cost(8192 * 128 * 256 * 2, 6 << 20, 1 << 20),
    )(rep, pair, weights)


def product_kernel(got_ref, out_ref, products, sems, *, by_row):
    def block(n, side):
        if by_row:
            return jnp.concatenate([got_ref[n, q, side] for q in range(8)], 1)
        return jnp.concatenate(
            [
                jnp.concatenate([got_ref[p, r, n, side] for r in range(8)], 1)
                for p in range(2)
            ],
            0,
        )

    copies = []
    for step in range(4):
        left = jnp.concatenate([block(2 * step, 0), block(2 * step + 1, 0)], 0)
        for q in range(0, 8, 2):
            right = jnp.concatenate([block(q, 1), block(q + 1, 1)], 0)
            hidden = lax.dot_general(right, left, NT, preferred_element_type=F32).astype(BF16)
            for qq in range(2):
                for p in range(2):
                    at = qq * 128 + p * 64
                    for r in range(2):
                        products[p, 2 * step + r, q + qq] = hidden[
                            at : at + 64, r * 128 : (r + 1) * 128
                        ]
        for p in range(2):
            rows = pl.ds(2 * step, 2)
            copy = pltpu.make_async_copy(
                products.at[p, rows], out_ref.at[p, rows], sems.at[step, p]
            )
            copy.start()
            copies.append(copy)
    for copy in copies:
        copy.wait()


def product(received, by_row):
    out = pl.pallas_call(
        functools.partial(product_kernel, by_row=by_row),
        name="product_out" if by_row else "product_in",
        in_specs=[VMEM],
        out_specs=ANY,
        out_shape=pltpu.HBM((2, 8, 8, 64, 128), BF16),
        scratch_shapes=[
            pltpu.VMEM((2, 8, 8, 64, 128), BF16),
            pltpu.SemaphoreType.DMA((4, 2)),
        ],
        compiler_params=params(PRODUCT_MIB),
        cost_estimate=cost(2 << 30, 6 << 20),
    )(received)
    return out.reshape(128, 64, 128)


def scale_hidden(hidden_ref, first, spread):
    total = jnp.zeros((ROWS, 128), F32)
    squares = jnp.zeros((ROWS, 128), F32)
    for c in range(128):
        values = hidden_ref[c, first : first + ROWS].astype(F32)
        total += values
        squares += values * values
    mean = total * (1.0 / 128)
    factor = lax.rsqrt(squares * (1.0 / 128) - mean * mean + epsilon)
    for c in range(128):
        spread[c * PITCH : c * PITCH + ROWS, :] = (
            hidden_ref[c, first : first + ROWS].astype(F32) - mean
        ) * factor
    return jnp.concatenate(
        [spread[pl.ds(r, 128, stride=PITCH), :] for r in range(ROWS)], 1
    ).astype(BF16)


def both_halves(rep_ref, mine, other):
    first = rep_ref[0] == 0
    return jnp.concatenate(
        [jnp.where(first, mine, other), jnp.where(first, other, mine)], 0
    )


def middle_kernel(
    rep_ref, hidden_ref, state_ref, gate_ref, mine_ref, other_ref, w_gate_ref, new_ref,
    new_gate_ref, out_ref, spread, sides, packed, old_state, old_gate, sems, load_sems,
):
    loads = []
    for first in range(0, 64, ROWS):
        part = pl.ds(first * 128, ROWS * 128)
        loads.append(
            [
                pltpu.make_async_copy(
                    source.at[:, part], target.at[:, part], load_sems.at[n, first // ROWS]
                )
                for n, (source, target) in enumerate(
                    ((state_ref, old_state), (gate_ref, old_gate))
                )
            ]
        )
    for pair_of_loads in loads:
        for load in pair_of_loads:
            load.start()
    w_out = both_halves(rep_ref, mine_ref[256:320], other_ref[256:320])
    weights = both_halves(rep_ref, mine_ref[:256], other_ref[:256])
    copies = []
    for first in range(0, 64, ROWS):
        where = slice(first * 128, (first + ROWS) * 128)
        scaled = scale_hidden(hidden_ref, first, spread)
        projected = lax.dot_general(w_out, scaled, TN, preferred_element_type=F32)
        for load in loads[first // ROWS]:
            load.wait()
        state = old_state[:, where].astype(F32) + old_gate[:, where].astype(F32) * projected
        new_ref[:, where] = state.astype(new_ref.dtype)
        normed = normalize(state).astype(BF16)
        half_gate = dot(w_gate_ref[...], normed)
        new_gate_ref[:, where] = (0.5 + 0.5 * jnp.tanh(half_gate)).astype(BF16)
        linear = dot(weights, normed)
        for half in range(2):
            at = half * 256
            left = gated(linear[at : at + 64], linear[at + 64 : at + 128])
            right = gated(linear[at + 128 : at + 192], linear[at + 192 : at + 256])
            for side, tile in enumerate((left, right)):
                for row in range(ROWS):
                    sides[side, pl.ds(half * 64 * PITCH + row, 64, stride=PITCH), :] = tile[
                        :, row * 128 : (row + 1) * 128
                    ]
        for side in range(2):
            for c in range(128):
                packed[c, side, first : first + ROWS] = sides[
                    side, c * PITCH : c * PITCH + ROWS, :
                ].astype(BF16)
        rows = pl.ds(first, ROWS)
        copy = pltpu.make_async_copy(
            packed.at[:, :, rows], out_ref.at[:, :, rows], sems.at[first // ROWS]
        )
        copy.start()
        copies.append(copy)
    for copy in copies:
        copy.wait()


def middle(rep, hidden, state, gate, mine, other, w_gate):
    return pl.pallas_call(
        middle_kernel,
        name="middle",
        in_specs=[SMEM, VMEM, ANY, ANY, VMEM, VMEM, VMEM],
        out_specs=[VMEM, VMEM, ANY],
        out_shape=[
            jax.ShapeDtypeStruct((128, 8192), BF16),
            jax.ShapeDtypeStruct((128, 8192), BF16),
            pltpu.HBM((128, 2, 64, 128), BF16),
        ],
        scratch_shapes=[
            pltpu.VMEM((128 * PITCH, 128), F32),
            pltpu.VMEM((2, 128 * PITCH, 128), F32),
            pltpu.VMEM((128, 2, 64, 128), BF16),
            pltpu.VMEM((128, 8192), BF16),
            pltpu.VMEM((128, 8192), BF16),
            pltpu.SemaphoreType.DMA((64 // ROWS,)),
            pltpu.SemaphoreType.DMA((2, 64 // ROWS)),
        ],
        compiler_params=params(MIDDLE_MIB),
        cost_estimate=cost(8192 * 128 * 640 * 2, 14 << 20, 1 << 21),
    )(rep, hidden, state, gate, mine, other, w_gate)


def finish_kernel(
    rep_ref, hidden_ref, state_ref, gate_ref, mine_ref, other_ref, w_in_ref, w_down_ref,
    out_ref, spread, state_scr, normed_scr, turned, packed, sems,
):
    w_out = both_halves(rep_ref, mine_ref[320:], other_ref[320:])
    w_half_gate = (w_in_ref[:512] * 0.5).astype(BF16)
    group = 8
    copies = []
    for first in range(0, 64, ROWS):
        where = slice(first * 128, (first + ROWS) * 128)
        scaled = scale_hidden(hidden_ref, first, spread)
        projected = lax.dot_general(w_out, scaled, TN, preferred_element_type=F32)
        state = state_ref[:, where].astype(F32) + gate_ref[:, where].astype(F32) * projected
        state_scr[...] = state
        normed_scr[...] = normalize(state).astype(BF16)
        for start in range(0, ROWS, group):
            part = slice(start * 128, (start + group) * 128)
            normed = normed_scr[:, part]
            half_gate = dot(w_half_gate, normed)
            linear = dot(w_in_ref[512:], normed)
            active = (gated(half_gate, half_gate) * linear).astype(BF16)
            updated = state_scr[:, part] + dot(w_down_ref[...], active)
            for row in range(group):
                turned[pl.ds(start + row, 128, stride=PITCH), :] = updated[
                    :, row * 128 : (row + 1) * 128
                ].T
        for i in range(128):
            packed[i, first : first + ROWS] = turned[i * PITCH : i * PITCH + ROWS, :].astype(
                BF16
            )
        rows = pl.ds(first, ROWS)
        copy = pltpu.make_async_copy(
            packed.at[:, rows], out_ref.at[:, rows], sems.at[first // ROWS]
        )
        copy.start()
        copies.append(copy)
    for copy in copies:
        copy.wait()


def finish(rep, hidden, state, gate, mine, other, w_in, w_down):
    return pl.pallas_call(
        finish_kernel,
        name="finish",
        in_specs=[SMEM] + [VMEM] * 7,
        out_specs=ANY,
        out_shape=pltpu.HBM((128, 64, 128), BF16),
        scratch_shapes=[
            pltpu.VMEM((128 * PITCH, 128), F32),
            pltpu.VMEM((128, ROWS * 128), F32),
            pltpu.VMEM((128, ROWS * 128), BF16),
            pltpu.VMEM((128 * PITCH, 128), F32),
            pltpu.VMEM((128, 64, 128), BF16),
            pltpu.SemaphoreType.DMA((64 // ROWS,)),
        ],
        compiler_params=params(FINISH_MIB),
        cost_estimate=cost(8192 * 128 * 1664 * 2, 10 << 20, 1 << 22),
    )(rep, hidden, state, gate, mine, other, w_in, w_down)


def exchange(values, axes):
    return lax.all_to_all(values, axes, split_axis=0, concat_axis=0, tiled=True)


def near(values):
    return pltpu.with_memory_space_constraint(values, pltpu.VMEM)


def far(values):
    return pltpu.with_memory_space_constraint(values, pltpu.HBM)


def on_device(
    pair, w_left, w_left_gate, w_right, w_right_gate, w_gate, w_out, w_trans_in, w_trans_out
):
    rep = lax.axis_index("rep").astype(jnp.int32).reshape(1)
    everywhere = ("rep", "row", "col")
    projections = [
        w.transpose(0, 2, 1) for w in (w_left, w_left_gate, w_right, w_right_gate)
    ]
    sides = front(pair, projections)
    sides, rep = lax.optimization_barrier((sides, rep))
    received = exchange(sides, ("row", "col"))

    products = product(near(received.reshape(8, 8, 2, 128, 128)), True)
    products, pair, w_gate, w_out, w_trans_in, w_trans_out, *projections = (
        lax.optimization_barrier(
            (products, pair, w_gate, w_out, w_trans_in, w_trans_out, *projections)
        )
    )
    hidden = exchange(products, everywhere)

    mine = jnp.concatenate(
        [(w[1] * 0.5).astype(BF16) for w in projections] + [w_out[0], w_out[1]], 0
    )
    other = lax.ppermute(mine, "rep", [(0, 1), (1, 0)])
    gates = (w_gate * 0.5).astype(BF16).transpose(0, 2, 1)
    w_in = w_trans_in.T
    w_down = w_trans_out.T
    state, gate = turn(rep, pair, gates[0])
    hidden, state, gate, gates, w_in, w_down, mine, other = lax.optimization_barrier(
        (hidden, state, gate, gates, w_in, w_down, mine, other)
    )

    state, gate, sides = middle(rep, near(hidden), far(state), far(gate), mine, other, gates[1])
    received = exchange(sides, everywhere)
    hidden = exchange(product(near(received.reshape(2, 8, 8, 2, 64, 128)), False), everywhere)
    return finish(rep, near(hidden), state, gate, mine, other, w_in, w_down)


def solution(mesh):
    placed = (
        P("row", "col", None),
        P(None, None, "rep"),
        P(None, None, "rep"),
        P(None, None, "rep"),
        P(None, None, "rep"),
        P(),
        P(None, "rep", None),
        P(),
        P(),
    )
    return jax.shard_map(
        on_device,
        mesh=mesh,
        in_specs=placed,
        out_specs=P("row", ("col", "rep"), None),
        check_vma=False,
    )
```

time: 234 us -> 226 us (0.966)
  blocking collectives: 71.4 us -> 156 us
  waiting for transfers between devices: 89.3 us -> 19.7 us
  Pallas kernels: 50.3 us -> 36.7 us
  starting transfers between devices: 20 us -> 8.94 us
    all_to_all x2 -> x3, blocking collectives: 71.4 us -> 156 us  [exchange(): return lax.all_to_all(values, axes, split_axis=0, concat_axis=0, tiled=True)]
    all_to_all x2 -> x1, waiting for transfers between devices: 47.1 us -> 2.04 us  [exchange(): return lax.all_to_all(values, axes, split_axis=0, concat_axis=0, tiled=True)]
    ppermute x1, waiting for transfers between devices: 42.2 us -> 17.7 us  [on_device(): other = lax.ppermute(mine, 'rep', [(0, 1), (1, 0)])]
    all_to_all x2 -> x1, starting transfers between devices: 17.5 us -> 5.79 us  [exchange(): return lax.all_to_all(values, axes, split_axis=0, concat_axis=0, tiled=True)]
    pallas_call x3 -> x2, Pallas kernels: 27.1 us -> 18.9 us  [the longest x1 10.4 us: finish(): pl.pallas_call(finish_kernel, name='finish', in_specs=[SMEM] + [VMEM] * 7...]
    pallas_call x2, Pallas kernels: 11 us -> 6.45 us  [product(): pl.pallas_call(functools.partial(product_kernel, by_row=by_row), name='pr...]
  transfers between devices with their start and end apart: 3 -> 2, of which waited for: 3 -> 2; matrix products, arithmetic and copies ran while one was open for 1% -> 0% of each run, Pallas kernels for 5% -> 2%
where the time goes in v3:
time: 226 us; the launch traced here: 225 us
  blocking collectives  156 us (69%)
  Pallas kernels  36.7 us (16%)
  waiting for transfers between devices  19.7 us (9%)
  starting transfers between devices  8.94 us (4%)
  local copies, waits for them, and re-layouts  2.67 us (1%)
    all_to_all x3, blocking collectives, exchange(): return lax.all_to_all(values, axes, split_axis=0, concat_axis=0, tiled=True)  156 us
    ppermute x1, waiting for transfers between devices, on_device(): other = lax.ppermute(mine, 'rep', [(0, 1), (1, 0)])  17.7 us
    pallas_call x1, Pallas kernels, finish(): pl.pallas_call(finish_kernel, name='finish', in_specs=[SMEM] + [VMEM] * 7...  10.4 us
    pallas_call x1, Pallas kernels, middle(): pl.pallas_call(middle_kernel, name='middle', in_specs=[SMEM, VMEM, ANY, A...  8.54 us
    pallas_call x1, Pallas kernels, front(): pl.pallas_call(front_kernel, name='front', grid=(128 // FRONT_ROWS,), in_...  7.49 us
    pallas_call x2, Pallas kernels, product(): pl.pallas_call(functools.partial(product_kernel, by_row=by_row), name='pr...  6.45 us
    all_to_all x1, starting transfers between devices, exchange(): return lax.all_to_all(values, axes, split_axis=0, concat_axis=0, tiled=True)  5.79 us
  transfers between devices with their start and end apart: 2, of which 2 were waited for; matrix products, arithmetic and copies ran while one was open for 0% of the time, Pallas kernels for 2%

profile of v3, /device:TPU:1, one launch (start us, length us, event | category | flops | bytes accessed | tf_op | source)
XLA Modules:
  0.0 224.9 jit_solution(16550813280615786835)
XLA Ops:
  0.0 7.5 %front.1 = bf16[64,2,128,128]{3,2,1,0:T(8,128)(2,1)} custom-call(bf16[128,128,128]{2,1,0:T(8,128)(2,1)} %pair_ref.2, bf16[2,64,128]{2,1,0:T(8,128)(2,1)} %bitcast.35, bf16[2,64,128]{2,1,0:T(8,128)(2,1)} %bitcast.37, bf16[2,64,128]{2,1,0:T(8,128)(2,1)} %bitcast.39, bf16[2,64,128]{2,1,0:T(8,128)(2,1)} %bitcast.41), custom_call_target="tpu_custom_call" | custom-call | flops 1610612736 | bytes 12582912 | tf_op jit(solution)/shard_map/front/pallas_call | solution.py:72
  7.5 61.9 %all_to_all.20 = bf16[64,2,128,128]{3,2,1,0:T(8,128)(2,1)S(1)} all-to-all(bf16[64,2,128,128]{3,2,1,0:T(8,128)(2,1)} %front.1), channel_id=1, replica_groups=mesh['row'=8,'col'=8,'rep'=2] {'row','col'}, dimensions={0} | all-to-all | bytes 8388608 | tf_op jit(solution)/shard_map/all_to_all | solution.py:345
  69.4 3.2 %product_out.1 = bf16[2,8,8,64,128]{4,3,2,1,0:T(8,128)(2,1)} custom-call(bf16[8,8,2,128,128]{4,3,2,1,0:T(8,128)(2,1)S(1)} %bitcast.29), custom_call_target="tpu_custom_call" | custom-call | flops 2147483648 | bytes 6291456 | tf_op jit(solution)/shard_map/product_out/pallas_call | solution.py:159
  72.6 0.0 copy-start.7
  72.6 0.0 copy-start.3
  72.6 0.0 copy-start.4
  72.6 0.0 copy-start.5
  72.7 0.0 copy-start.6
  72.7 0.0 copy-start.8
  72.7 0.0 copy-start.2
  72.7 0.0 copy-start.1
  72.7 5.8 %all-to-all-start.1 = ((bf16[128,64,128]{2,1,0:T(8,128)(2,1)}), bf16[128,64,128]{2,1,0:T(8,128)(2,1)S(1)}, u32[]{:S(2)}, u32[]{:S(2)}) async-start(bf16[128,64,128]{2,1,0:T(8,128)(2,1)} %bitcast.33), calls=%async_computation.1 | async-start | bytes 4194304 | tf_op jit(solution)/shard_map/all_to_all | solution.py:345
  78.5 0.0 copy-done.7
  78.5 0.1 copy.10
  78.6 0.0 copy-done.3
  78.7 0.0 copy-done.4
  78.7 0.0 copy-done.5
  78.7 0.0 copy-done.6
  78.7 0.0 copy-done.8
  78.8 3.2 %collective-permute-start = (bf16[384,128]{1,0:T(8,128)(2,1)S(1)}, bf16[384,128]{1,0:T(8,128)(2,1)S(1)}, u32[]{:S(2)}, u32[]{:S(2)}) collective-permute-start(bf16[384,128]{1,0:T(8,128)(2,1)S(1)} %bitcast_dynamic-update-slice_fusion.mine_ref), channel_id=1, source_target_pairs={{0,1},{1,0},{2,3},{3,2},{4,5},{5,4},{6,7},{7,6},{8,9},{9,8},{10,11... | collective-permute-start | bytes 294920 | tf_op jit(solution)/shard_map/ppermute | solution.py:379
  82.0 0.0 copy-done.2
  82.0 0.1 copy.12
  82.1 0.0 copy-done.1
  82.1 0.2 copy.11
  82.3 0.0 copy-start
  82.3 2.2 copy-done
  84.5 3.9 %turn.1 = (bf16[128,8192]{1,0:T(8,128)(2,1)}, bf16[128,8192]{1,0:T(8,128)(2,1)}) custom-call(s32[1]{0:T(128)} %bitcast.4.rep_ref, bf16[128,128,128]{2,1,0:T(8,128)(2,1)S(1)} %copy-done, bf16[128,128]{1,0:T(8,128)(2,1)S(1)} %slice_bitcast_fusion.w_ref), custom_call_target="tpu_custom_call" | custom-call | flops 536870912 | bytes 6291456 | tf_op jit(solution)/shard_map/turn/pallas_call | solution.py:103
  88.4 17.7 %collective-permute-done.other_ref = bf16[384,128]{1,0:T(8,128)(2,1)S(1)} collective-permute-done((bf16[384,128]{1,0:T(8,128)(2,1)S(1)}, bf16[384,128]{1,0:T(8,128)(2,1)S(1)}, u32[]{:S(2)}, u32[]{:S(2)}) %collective-permute-start) | collective-permute-done | bytes 98336 | tf_op jit(solution)/shard_map/ppermute | solution.py:379
  106.1 2.0 all-to-all-done.1.hidden_ref
  108.1 8.5 %middle.1 = (bf16[128,8192]{1,0:T(8,128)(2,1)S(1)}, bf16[128,8192]{1,0:T(8,128)(2,1)S(1)}, bf16[128,2,64,128]{3,2,1,0:T(8,128)(2,1)}) custom-call(s32[1]{0:T(128)} %bitcast.4.rep_ref, bf16[128,64,128]{2,1,0:T(8,128)(2,1)S(1)} %all-to-all-done.1.hidden_ref, bf16[128,8192]{1,0:T(8,128)(2,1)} %get-tuple-element.45.state_ref, ...), custom_call_target="tpu_custom_call" | custom-call | flops 1342177280 | bytes 14680064 | tf_op jit(solution)/shard_map/middle/pallas_call | solution.py:260
  116.7 58.1 %all_to_all.21 = bf16[128,2,64,128]{3,2,1,0:T(8,128)(2,1)S(1)} all-to-all(bf16[128,2,64,128]{3,2,1,0:T(8,128)(2,1)} %get-tuple-element.50), channel_id=1, replica_groups=mesh['row'=8,'col'=8,'rep'=2] {'rep','row','col'}, dimensions={0} | all-to-all | bytes 8388608 | tf_op jit(solution)/shard_map/all_to_all | solution.py:345
  174.7 3.2 %product_in.1 = bf16[2,8,8,64,128]{4,3,2,1,0:T(8,128)(2,1)} custom-call(bf16[2,8,8,2,64,128]{5,4,3,2,1,0:T(8,128)(2,1)S(1)} %bitcast.30), custom_call_target="tpu_custom_call" | custom-call | flops 2147483648 | bytes 6291456 | tf_op jit(solution)/shard_map/product_in/pallas_call | solution.py:159
  178.0 36.5 %all_to_all.22.hidden_ref = bf16[128,64,128]{2,1,0:T(8,128)(2,1)S(1)} all-to-all(bf16[128,64,128]{2,1,0:T(8,128)(2,1)} %bitcast.34), channel_id=1, replica_groups=mesh['row'=8,'col'=8,'rep'=2] {'rep','row','col'}, dimensions={0} | all-to-all | bytes 4194304 | tf_op jit(solution)/shard_map/all_to_all | solution.py:345
  214.4 10.4 %finish.1 = bf16[128,64,128]{2,1,0:T(8,128)(2,1)} custom-call(s32[1]{0:T(128)} %bitcast.4.rep_ref, bf16[128,64,128]{2,1,0:T(8,128)(2,1)S(1)} %all_to_all.22.hidden_ref, bf16[128,8192]{1,0:T(8,128)(2,1)S(1)} %get-tuple-element.51.state_ref, bf16[128,8192]{1,0:T(8,128)(2,1)S(1)} %get-tuple-element.52.gate_ref, ...), custom_call_target="tpu_custom_call" | custom-call | flops 3489660928 | bytes 10485760 | tf_op jit(solution)/shard_map/finish/pallas_call | solution.py:325
  (9 shorter events, 0.1 us)
Async XLA Ops:
  72.6 5.9 %copy-start.7 = (bf16[2,128,128]{2,1,0:T(8,128)(2,1)S(1)}, bf16[2,128,128]{2,1,0:T(8,128)(2,1)}, u32[]{:S(2)}) copy-start(bf16[2,128,128]{2,1,0:T(8,128)(2,1)} %param.14) | copy-start | bytes 196612
  72.6 6.0 %copy-start.3 = (bf16[2,128,64]{1,2,0:T(8,128)(2,1)S(1)}, bf16[2,128,64]{1,2,0:T(8,128)(2,1)}, u32[]{:S(2)}) copy-start(bf16[2,128,64]{1,2,0:T(8,128)(2,1)} %param.10) | copy-start | bytes 98308
  72.6 6.0 %copy-start.4 = (bf16[2,128,64]{1,2,0:T(8,128)(2,1)S(1)}, bf16[2,128,64]{1,2,0:T(8,128)(2,1)}, u32[]{:S(2)}) copy-start(bf16[2,128,64]{1,2,0:T(8,128)(2,1)} %param.11) | copy-start | bytes 98308
  72.6 6.0 %copy-start.5 = (bf16[2,128,64]{1,2,0:T(8,128)(2,1)S(1)}, bf16[2,128,64]{1,2,0:T(8,128)(2,1)}, u32[]{:S(2)}) copy-start(bf16[2,128,64]{1,2,0:T(8,128)(2,1)} %param.12) | copy-start | bytes 98308
  72.7 6.1 %copy-start.6 = (bf16[2,128,64]{1,2,0:T(8,128)(2,1)S(1)}, bf16[2,128,64]{1,2,0:T(8,128)(2,1)}, u32[]{:S(2)}) copy-start(bf16[2,128,64]{1,2,0:T(8,128)(2,1)} %param.13) | copy-start | bytes 98308
  72.7 6.1 %copy-start.8 = (bf16[2,64,128]{2,1,0:T(8,128)(2,1)S(1)}, bf16[2,64,128]{2,1,0:T(8,128)(2,1)}, u32[]{:S(2)}) copy-start(bf16[2,64,128]{2,1,0:T(8,128)(2,1)} %param.15) | copy-start | bytes 98308
  72.7 9.3 %copy-start.2 = (bf16[512,128]{1,0:T(8,128)(2,1)S(1)}, bf16[512,128]{1,0:T(8,128)(2,1)}, u32[]{:S(2)}) copy-start(bf16[512,128]{1,0:T(8,128)(2,1)} %param.17) | copy-start | bytes 393220
  72.7 9.4 %copy-start.1 = (bf16[128,1024]{1,0:T(8,128)(2,1)S(1)}, bf16[128,1024]{1,0:T(8,128)(2,1)}, u32[]{:S(2)}) copy-start(bf16[128,1024]{1,0:T(8,128)(2,1)} %param.16) | copy-start | bytes 786436
  72.7 35.4 %all-to-all-start.1 = ((bf16[128,64,128]{2,1,0:T(8,128)(2,1)}), bf16[128,64,128]{2,1,0:T(8,128)(2,1)S(1)}, u32[]{:S(2)}, u32[]{:S(2)}) async-start(bf16[128,64,128]{2,1,0:T(8,128)(2,1)} %bitcast.33), calls=%async_computation.1 | async-start | bytes 4194304 | tf_op jit(solution)/shard_map/all_to_all | solution.py:345
  78.8 27.3 %collective-permute-start = (bf16[384,128]{1,0:T(8,128)(2,1)S(1)}, bf16[384,128]{1,0:T(8,128)(2,1)S(1)}, u32[]{:S(2)}, u32[]{:S(2)}) collective-permute-start(bf16[384,128]{1,0:T(8,128)(2,1)S(1)} %bitcast_dynamic-update-slice_fusion.mine_ref), channel_id=1, source_target_pairs={{0,1},{1,0},{2,3},{3,2},{4,5},{5,4},{6,7},{7,6},{8,9},{9,8},{10,11... | collective-permute-start | bytes 294920 | tf_op jit(solution)/shard_map/ppermute | solution.py:379
  82.3 2.2 copy-start

commit v4 on v3

--- a/solution.py
+++ b/solution.py
@@ -19,7 +19,7 @@
 FRONT_ROWS, FRONT_PITCH = 32, 33
 
 
-PRODUCT_MIB, MIDDLE_MIB, FINISH_MIB = 24, 36, 36
+FRONT_MIB, PRODUCT_MIB, MIDDLE_MIB, FINISH_MIB = 36, 24, 36, 36
 
 
 def params(mebibytes):
@@ -46,41 +46,67 @@
     return jnp.dot(a, b, preferred_element_type=F32)
 
 
-def front_kernel(pair_ref, wl_ref, wlg_ref, wr_ref, wrg_ref, out_ref, spread):
-    weights = jnp.concatenate([wl_ref[0], wlg_ref[0], wr_ref[0], wrg_ref[0]], 0) * 0.5
-    weights = weights.astype(BF16)
+def front_kernel(
+    pair_ref, wl_ref, wlg_ref, wr_ref, wrg_ref, out_ref, rows_in, weights_in, spread, sems, w_sems
+):
+    loads = []
+    for step in range(128 // FRONT_ROWS):
+        rows = pl.ds(step * FRONT_ROWS, FRONT_ROWS)
+        loads.append(
+            pltpu.make_async_copy(pair_ref.at[rows], rows_in.at[rows], sems.at[step])
+        )
+    w_loads = [
+        pltpu.make_async_copy(ref.at[0], weights_in.at[pl.ds(64 * n, 64)], w_sems.at[n])
+        for n, ref in enumerate((wl_ref, wlg_ref, wr_ref, wrg_ref))
+    ]
+    for load in w_loads + loads[:2]:
+        load.start()
+    for load in w_loads:
+        load.wait()
+    weights = (weights_in[...] * 0.5).astype(BF16)
     group = 4
-    for first in range(0, FRONT_ROWS, group):
-        state = jnp.concatenate(
-            [pair_ref[first + row].T for row in range(group)], 1
-        ).astype(F32)
-        linear = dot(weights, normalize(state).astype(BF16))
-        left = gated(linear[0:64], linear[64:128])
-        right = gated(linear[128:192], linear[192:256])
-        for side, tile in enumerate((left, right)):
-            for row in range(group):
-                spread[side, pl.ds(first + row, 64, stride=FRONT_PITCH), :] = tile[
-                    :, row * 128 : (row + 1) * 128
-                ]
-    for side in range(2):
-        for c in range(64):
-            at = c * FRONT_PITCH
-            out_ref[c, side] = spread[side, at : at + FRONT_ROWS, :].astype(BF16)
+    for step, load in enumerate(loads):
+        load.wait()
+        if step + 2 < len(loads):
+            loads[step + 2].start()
+        start = step * FRONT_ROWS
+        for first in range(0, FRONT_ROWS, group):
+            state = jnp.concatenate(
+                [rows_in[start + first + row].T for row in range(group)], 1
+            ).astype(F32)
+            linear = dot(weights, normalize(state).astype(BF16))
+            left = gated(linear[0:64], linear[64:128])
+            right = gated(linear[128:192], linear[192:256])
+            for side, tile in enumerate((left, right)):
+                for row in range(group):
+                    spread[side, pl.ds(first + row, 64, stride=FRONT_PITCH), :] = tile[
+                        :, row * 128 : (row + 1) * 128
+                    ]
+        for side in range(2):
+            for c in range(64):
+                at = c * FRONT_PITCH
+                out_ref[c, side, start : start + FRONT_ROWS] = spread[
+                    side, at : at + FRONT_ROWS, :
+                ].astype(BF16)
 
 
 def front(pair, weights):
     return pl.pallas_call(
         front_kernel,
         name="front",
-        grid=(128 // FRONT_ROWS,),
-        in_specs=[pl.BlockSpec((FRONT_ROWS, 128, 128), lambda s: (s, 0, 0))]
-        + [pl.BlockSpec((1, 64, 128), lambda s: (0, 0, 0))] * 4,
-        out_specs=pl.BlockSpec((64, 2, FRONT_ROWS, 128), lambda s: (0, 0, s, 0)),
-        out_shape=pltpu.HBM((64, 2, 128, 128), BF16),
-        scratch_shapes=[pltpu.VMEM((2, 64 * FRONT_PITCH, 128), F32)],
-        compiler_params=params(60),
+        in_specs=[ANY] * 5,
+        out_specs=VMEM,
+        out_shape=pltpu.VMEM((64, 2, 128, 128), BF16),
+        scratch_shapes=[
+            pltpu.VMEM((128, 128, 128), BF16),
+            pltpu.VMEM((256, 128), BF16),
+            pltpu.VMEM((2, 64 * FRONT_PITCH, 128), F32),
+            pltpu.SemaphoreType.DMA((128 // FRONT_ROWS,)),
+            pltpu.SemaphoreType.DMA((4,)),
+        ],
+        compiler_params=params(FRONT_MIB),
         cost_estimate=cost(16384 * 128 * 384 * 2, 12 << 20, 1 << 21),
-    )(pair, *weights)
+    )(far(pair), *[far(w) for w in weights])
 
 
 def turn_kernel(rep_ref, pair_ref, w_ref, state_ref, gate_ref, spread):
@@ -119,7 +145,7 @@
     )(rep, pair, weights)
 
 
-def product_kernel(got_ref, out_ref, products, sems, *, by_row):
+def product_kernel(got_ref, out_ref, *scratch, by_row):
     def block(n, side):
         if by_row:
             return jnp.concatenate([got_ref[n, q, side] for q in range(8)], 1)
@@ -131,6 +157,7 @@
             0,
         )
 
+    products = scratch[0] if by_row else out_ref
     copies = []
     for step in range(4):
         left = jnp.concatenate([block(2 * step, 0), block(2 * step + 1, 0)], 0)
@@ -144,10 +171,10 @@
                         products[p, 2 * step + r, q + qq] = hidden[
                             at : at + 64, r * 128 : (r + 1) * 128
                         ]
-        for p in range(2):
+        for p in range(2 if by_row else 0):
             rows = pl.ds(2 * step, 2)
             copy = pltpu.make_async_copy(
-                products.at[p, rows], out_ref.at[p, rows], sems.at[step, p]
+                products.at[p, rows], out_ref.at[p, rows], scratch[1].at[step, p]
             )
             copy.start()
             copies.append(copy)
@@ -160,12 +187,14 @@
         functools.partial(product_kernel, by_row=by_row),
         name="product_out" if by_row else "product_in",
         in_specs=[VMEM],
-        out_specs=ANY,
-        out_shape=pltpu.HBM((2, 8, 8, 64, 128), BF16),
+        out_specs=ANY if by_row else VMEM,
+        out_shape=(pltpu.HBM if by_row else pltpu.VMEM)((2, 8, 8, 64, 128), BF16),
         scratch_shapes=[
             pltpu.VMEM((2, 8, 8, 64, 128), BF16),
             pltpu.SemaphoreType.DMA((4, 2)),
-        ],
+        ]
+        if by_row
+        else [],
         compiler_params=params(PRODUCT_MIB),
         cost_estimate=cost(2 << 30, 6 << 20),
     )(received)
@@ -199,7 +228,7 @@
 
 def middle_kernel(
     rep_ref, hidden_ref, state_ref, gate_ref, mine_ref, other_ref, w_gate_ref, new_ref,
-    new_gate_ref, out_ref, spread, sides, packed, old_state, old_gate, sems, load_sems,
+    new_gate_ref, out_ref, spread, sides, old_state, old_gate, load_sems,
 ):
     loads = []
     for first in range(0, 64, ROWS):
@@ -214,18 +243,20 @@
                 )
             ]
         )
-    for pair_of_loads in loads:
-        for load in pair_of_loads:
-            load.start()
+    for load in loads[0] + loads[1]:
+        load.start()
     w_out = both_halves(rep_ref, mine_ref[256:320], other_ref[256:320])
     weights = both_halves(rep_ref, mine_ref[:256], other_ref[:256])
-    copies = []
     for first in range(0, 64, ROWS):
         where = slice(first * 128, (first + ROWS) * 128)
         scaled = scale_hidden(hidden_ref, first, spread)
         projected = lax.dot_general(w_out, scaled, TN, preferred_element_type=F32)
-        for load in loads[first // ROWS]:
+        step = first // ROWS
+        for load in loads[step]:
             load.wait()
+        if step + 2 < len(loads):
+            for load in loads[step + 2]:
+                load.start()
         state = old_state[:, where].astype(F32) + old_gate[:, where].astype(F32) * projected
         new_ref[:, where] = state.astype(new_ref.dtype)
         normed = normalize(state).astype(BF16)
@@ -243,17 +274,9 @@
                     ]
         for side in range(2):
             for c in range(128):
-                packed[c, side, first : first + ROWS] = sides[
+                out_ref[c, side, first : first + ROWS] = sides[
                     side, c * PITCH : c * PITCH + ROWS, :
                 ].astype(BF16)
-        rows = pl.ds(first, ROWS)
-        copy = pltpu.make_async_copy(
-            packed.at[:, :, rows], out_ref.at[:, :, rows], sems.at[first // ROWS]
-        )
-        copy.start()
-        copies.append(copy)
-    for copy in copies:
-        copy.wait()
 
 
 def middle(rep, hidden, state, gate, mine, other, w_gate):
@@ -261,19 +284,17 @@
         middle_kernel,
         name="middle",
         in_specs=[SMEM, VMEM, ANY, ANY, VMEM, VMEM, VMEM],
-        out_specs=[VMEM, VMEM, ANY],
+        out_specs=[VMEM, VMEM, VMEM],
         out_shape=[
             jax.ShapeDtypeStruct((128, 8192), BF16),
             jax.ShapeDtypeStruct((128, 8192), BF16),
-            pltpu.HBM((128, 2, 64, 128), BF16),
+            pltpu.VMEM((128, 2, 64, 128), BF16),
         ],
         scratch_shapes=[
             pltpu.VMEM((128 * PITCH, 128), F32),
             pltpu.VMEM((2, 128 * PITCH, 128), F32),
-            pltpu.VMEM((128, 2, 64, 128), BF16),
             pltpu.VMEM((128, 8192), BF16),
             pltpu.VMEM((128, 8192), BF16),
-            pltpu.SemaphoreType.DMA((64 // ROWS,)),
             pltpu.SemaphoreType.DMA((2, 64 // ROWS)),
         ],
         compiler_params=params(MIDDLE_MIB),

time: 226 us -> 222 us (0.982)
  Pallas kernels: 36.7 us -> 33.4 us
where the time goes in v4:
time: 222 us; the launch traced here: 221 us
  blocking collectives  156 us (70%)
  Pallas kernels  33.4 us (15%)
  waiting for transfers between devices  19.7 us (9%)
  starting transfers between devices  8.95 us (4%)
  local copies, waits for them, and re-layouts  2.67 us (1%)
    all_to_all x3, blocking collectives, exchange(): return lax.all_to_all(values, axes, split_axis=0, concat_axis=0, tiled=True)  156 us
    ppermute x1, waiting for transfers between devices, on_device(): other = lax.ppermute(mine, 'rep', [(0, 1), (1, 0)])  17.7 us
    pallas_call x1, Pallas kernels, finish(): pl.pallas_call(finish_kernel, name='finish', in_specs=[SMEM] + [VMEM] * 7...  10.4 us
    pallas_call x1, Pallas kernels, middle(): pl.pallas_call(middle_kernel, name='middle', in_specs=[SMEM, VMEM, ANY, A...  7.47 us
    pallas_call x1, Pallas kernels, front(): pl.pallas_call(front_kernel, name='front', in_specs=[ANY] * 5, out_specs=...  6.08 us
    all_to_all x1, starting transfers between devices, exchange(): return lax.all_to_all(values, axes, split_axis=0, concat_axis=0, tiled=True)  5.8 us
    pallas_call x2, Pallas kernels, product(): pl.pallas_call(functools.partial(product_kernel, by_row=by_row), name='pr...  5.59 us
  transfers between devices with their start and end apart: 2, of which 2 were waited for; matrix products, arithmetic and copies ran while one was open for 0% of the time, Pallas kernels for 2%

profile of v4, /device:TPU:1, one launch (start us, length us, event | category | flops | bytes accessed | tf_op | source)
XLA Modules:
  0.0 221.0 jit_solution(5866793837277476958)
XLA Ops:
  0.0 6.1 %front.1 = bf16[64,2,128,128]{3,2,1,0:T(8,128)(2,1)S(1)} custom-call(bf16[128,128,128]{2,1,0:T(8,128)(2,1)} %pair_ref.2, bf16[2,64,128]{2,1,0:T(8,128)(2,1)} %bitcast.35, bf16[2,64,128]{2,1,0:T(8,128)(2,1)} %bitcast.37, bf16[2,64,128]{2,1,0:T(8,128)(2,1)} %bitcast.39, bf16[2,64,128]{2,1,0:T(8,128)(2,1)} %bitcast.41), custom_call_target="tpu_custom_call" | custom-call | flops 1610612736 | bytes 12582912 | tf_op jit(solution)/shard_map/front/pallas_call | solution.py:94
  6.1 61.7 %all_to_all.20 = bf16[64,2,128,128]{3,2,1,0:T(8,128)(2,1)S(1)} all-to-all(bf16[64,2,128,128]{3,2,1,0:T(8,128)(2,1)S(1)} %front.1), channel_id=1, replica_groups=mesh['row'=8,'col'=8,'rep'=2] {'row','col'}, dimensions={0} | all-to-all | bytes 8388608 | tf_op jit(solution)/shard_map/all_to_all | solution.py:366
  67.8 3.2 %product_out.1 = bf16[2,8,8,64,128]{4,3,2,1,0:T(8,128)(2,1)} custom-call(bf16[8,8,2,128,128]{4,3,2,1,0:T(8,128)(2,1)S(1)} %bitcast.29), custom_call_target="tpu_custom_call" | custom-call | flops 2147483648 | bytes 6291456 | tf_op jit(solution)/shard_map/product_out/pallas_call | solution.py:186
  71.0 0.0 copy-start.7
  71.0 0.0 copy-start.3
  71.0 0.0 copy-start.4
  71.0 0.0 copy-start.5
  71.0 0.0 copy-start.6
  71.1 0.0 copy-start.8
  71.1 0.0 copy-start.2
  71.1 0.0 copy-start.1
  71.1 5.8 %all-to-all-start.1 = ((bf16[128,64,128]{2,1,0:T(8,128)(2,1)}), bf16[128,64,128]{2,1,0:T(8,128)(2,1)S(1)}, u32[]{:S(2)}, u32[]{:S(2)}) async-start(bf16[128,64,128]{2,1,0:T(8,128)(2,1)} %bitcast.34), calls=%async_computation.1 | async-start | bytes 4194304 | tf_op jit(solution)/shard_map/all_to_all | solution.py:366
  76.9 0.0 copy-done.7
  76.9 0.1 copy.10
  77.0 0.0 copy-done.3
  77.1 0.0 copy-done.4
  77.1 0.0 copy-done.5
  77.1 0.0 copy-done.6
  77.1 0.0 copy-done.8
  77.2 3.2 %collective-permute-start = (bf16[384,128]{1,0:T(8,128)(2,1)S(1)}, bf16[384,128]{1,0:T(8,128)(2,1)S(1)}, u32[]{:S(2)}, u32[]{:S(2)}) collective-permute-start(bf16[384,128]{1,0:T(8,128)(2,1)S(1)} %bitcast_dynamic-update-slice_fusion.mine_ref), channel_id=1, source_target_pairs={{0,1},{1,0},{2,3},{3,2},{4,5},{5,4},{6,7},{7,6},{8,9},{9,8},{10,11... | collective-permute-start | bytes 294920 | tf_op jit(solution)/shard_map/ppermute | solution.py:400
  80.3 0.0 copy-done.2
  80.4 0.1 copy.12
  80.5 0.0 copy-done.1
  80.5 0.2 copy.11
  80.7 0.0 copy-start
  80.7 2.2 copy-done
  82.9 3.9 %turn.1 = (bf16[128,8192]{1,0:T(8,128)(2,1)}, bf16[128,8192]{1,0:T(8,128)(2,1)}) custom-call(s32[1]{0:T(128)} %bitcast.4.rep_ref, bf16[128,128,128]{2,1,0:T(8,128)(2,1)S(1)} %copy-done, bf16[128,128]{1,0:T(8,128)(2,1)S(1)} %slice_bitcast_fusion.w_ref), custom_call_target="tpu_custom_call" | custom-call | flops 536870912 | bytes 6291456 | tf_op jit(solution)/shard_map/turn/pallas_call | solution.py:129
  86.8 17.7 %collective-permute-done.other_ref = bf16[384,128]{1,0:T(8,128)(2,1)S(1)} collective-permute-done((bf16[384,128]{1,0:T(8,128)(2,1)S(1)}, bf16[384,128]{1,0:T(8,128)(2,1)S(1)}, u32[]{:S(2)}, u32[]{:S(2)}) %collective-permute-start) | collective-permute-done | bytes 98336 | tf_op jit(solution)/shard_map/ppermute | solution.py:400
  104.5 2.0 all-to-all-done.1.hidden_ref
  106.5 7.5 %middle.1 = (bf16[128,8192]{1,0:T(8,128)(2,1)S(1)}, bf16[128,8192]{1,0:T(8,128)(2,1)S(1)}, bf16[128,2,64,128]{3,2,1,0:T(8,128)(2,1)S(1)}) custom-call(s32[1]{0:T(128)} %bitcast.4.rep_ref, bf16[128,64,128]{2,1,0:T(8,128)(2,1)S(1)} %all-to-all-done.1.hidden_ref, bf16[128,8192]{1,0:T(8,128)(2,1)} %get-tuple-element.45.state_ref, ...), custom_call_target="tpu_custom_call" | custom-call | flops 1342177280 | bytes 14680064 | tf_op jit(solution)/shard_map/middle/pallas_call | solution.py:283
  114.0 57.9 %all_to_all.21 = bf16[128,2,64,128]{3,2,1,0:T(8,128)(2,1)S(1)} all-to-all(bf16[128,2,64,128]{3,2,1,0:T(8,128)(2,1)S(1)} %get-tuple-element.50), channel_id=1, replica_groups=mesh['row'=8,'col'=8,'rep'=2] {'rep','row','col'}, dimensions={0} | all-to-all | bytes 8388608 | tf_op jit(solution)/shard_map/all_to_all | solution.py:366
  171.8 2.4 %product_in.1 = bf16[2,8,8,64,128]{4,3,2,1,0:T(8,128)(2,1)S(1)} custom-call(bf16[2,8,8,2,64,128]{5,4,3,2,1,0:T(8,128)(2,1)S(1)} %bitcast.30), custom_call_target="tpu_custom_call" | custom-call | flops 2147483648 | bytes 6291456 | tf_op jit(solution)/shard_map/product_in/pallas_call | solution.py:186
  174.2 36.2 %all_to_all.22.hidden_ref = bf16[128,64,128]{2,1,0:T(8,128)(2,1)S(1)} all-to-all(bf16[128,64,128]{2,1,0:T(8,128)(2,1)S(1)} %bitcast.31), channel_id=1, replica_groups=mesh['row'=8,'col'=8,'rep'=2] {'rep','row','col'}, dimensions={0} | all-to-all | bytes 4194304 | tf_op jit(solution)/shard_map/all_to_all | solution.py:366
  210.4 10.4 %finish.1 = bf16[128,64,128]{2,1,0:T(8,128)(2,1)} custom-call(s32[1]{0:T(128)} %bitcast.4.rep_ref, bf16[128,64,128]{2,1,0:T(8,128)(2,1)S(1)} %all_to_all.22.hidden_ref, bf16[128,8192]{1,0:T(8,128)(2,1)S(1)} %get-tuple-element.51.state_ref, bf16[128,8192]{1,0:T(8,128)(2,1)S(1)} %get-tuple-element.52.gate_ref, ...), custom_call_target="tpu_custom_call" | custom-call | flops 3489660928 | bytes 10485760 | tf_op jit(solution)/shard_map/finish/pallas_call | solution.py:346
  (9 shorter events, 0.1 us)
Async XLA Ops:
  71.0 5.9 %copy-start.7 = (bf16[2,128,128]{2,1,0:T(8,128)(2,1)S(1)}, bf16[2,128,128]{2,1,0:T(8,128)(2,1)}, u32[]{:S(2)}) copy-start(bf16[2,128,128]{2,1,0:T(8,128)(2,1)} %param.14) | copy-start | bytes 196612
  71.0 6.0 %copy-start.3 = (bf16[2,128,64]{1,2,0:T(8,128)(2,1)S(1)}, bf16[2,128,64]{1,2,0:T(8,128)(2,1)}, u32[]{:S(2)}) copy-start(bf16[2,128,64]{1,2,0:T(8,128)(2,1)} %param.10) | copy-start | bytes 98308
  71.0 6.0 %copy-start.4 = (bf16[2,128,64]{1,2,0:T(8,128)(2,1)S(1)}, bf16[2,128,64]{1,2,0:T(8,128)(2,1)}, u32[]{:S(2)}) copy-start(bf16[2,128,64]{1,2,0:T(8,128)(2,1)} %param.11) | copy-start | bytes 98308
  71.0 6.1 %copy-start.5 = (bf16[2,128,64]{1,2,0:T(8,128)(2,1)S(1)}, bf16[2,128,64]{1,2,0:T(8,128)(2,1)}, u32[]{:S(2)}) copy-start(bf16[2,128,64]{1,2,0:T(8,128)(2,1)} %param.12) | copy-start | bytes 98308
  71.0 6.1 %copy-start.6 = (bf16[2,128,64]{1,2,0:T(8,128)(2,1)S(1)}, bf16[2,128,64]{1,2,0:T(8,128)(2,1)}, u32[]{:S(2)}) copy-start(bf16[2,128,64]{1,2,0:T(8,128)(2,1)} %param.13) | copy-start | bytes 98308
  71.1 6.1 %copy-start.8 = (bf16[2,64,128]{2,1,0:T(8,128)(2,1)S(1)}, bf16[2,64,128]{2,1,0:T(8,128)(2,1)}, u32[]{:S(2)}) copy-start(bf16[2,64,128]{2,1,0:T(8,128)(2,1)} %param.15) | copy-start | bytes 98308
  71.1 9.3 %copy-start.2 = (bf16[512,128]{1,0:T(8,128)(2,1)S(1)}, bf16[512,128]{1,0:T(8,128)(2,1)}, u32[]{:S(2)}) copy-start(bf16[512,128]{1,0:T(8,128)(2,1)} %param.17) | copy-start | bytes 393220
  71.1 9.4 %copy-start.1 = (bf16[128,1024]{1,0:T(8,128)(2,1)S(1)}, bf16[128,1024]{1,0:T(8,128)(2,1)}, u32[]{:S(2)}) copy-start(bf16[128,1024]{1,0:T(8,128)(2,1)} %param.16) | copy-start | bytes 786436
  71.1 35.4 %all-to-all-start.1 = ((bf16[128,64,128]{2,1,0:T(8,128)(2,1)}), bf16[128,64,128]{2,1,0:T(8,128)(2,1)S(1)}, u32[]{:S(2)}, u32[]{:S(2)}) async-start(bf16[128,64,128]{2,1,0:T(8,128)(2,1)} %bitcast.34), calls=%async_computation.1 | async-start | bytes 4194304 | tf_op jit(solution)/shard_map/all_to_all | solution.py:366
  77.2 27.3 %collective-permute-start = (bf16[384,128]{1,0:T(8,128)(2,1)S(1)}, bf16[384,128]{1,0:T(8,128)(2,1)S(1)}, u32[]{:S(2)}, u32[]{:S(2)}) collective-permute-start(bf16[384,128]{1,0:T(8,128)(2,1)S(1)} %bitcast_dynamic-update-slice_fusion.mine_ref), channel_id=1, source_target_pairs={{0,1},{1,0},{2,3},{3,2},{4,5},{5,4},{6,7},{7,6},{8,9},{9,8},{10,11... | collective-permute-start | bytes 294920 | tf_op jit(solution)/shard_map/ppermute | solution.py:400
  80.7 2.2 copy-start

commit v5 on v4

--- a/solution.py
+++ b/solution.py
@@ -151,7 +151,7 @@
             return jnp.concatenate([got_ref[n, q, side] for q in range(8)], 1)
         return jnp.concatenate(
             [
-                jnp.concatenate([got_ref[p, r, n, side] for r in range(8)], 1)
+                jnp.concatenate([got_ref[r, p, n, side] for r in range(8)], 1)
                 for p in range(2)
             ],
             0,
@@ -168,13 +168,13 @@
                 for p in range(2):
                     at = qq * 128 + p * 64
                     for r in range(2):
-                        products[p, 2 * step + r, q + qq] = hidden[
+                        products[2 * step + r, p, q + qq] = hidden[
                             at : at + 64, r * 128 : (r + 1) * 128
                         ]
-        for p in range(2 if by_row else 0):
+        if by_row:
             rows = pl.ds(2 * step, 2)
             copy = pltpu.make_async_copy(
-                products.at[p, rows], out_ref.at[p, rows], scratch[1].at[step, p]
+                products.at[rows], out_ref.at[rows], scratch[1].at[step]
             )
             copy.start()
             copies.append(copy)
@@ -188,10 +188,10 @@
         name="product_out" if by_row else "product_in",
         in_specs=[VMEM],
         out_specs=ANY if by_row else VMEM,
-        out_shape=(pltpu.HBM if by_row else pltpu.VMEM)((2, 8, 8, 64, 128), BF16),
+        out_shape=(pltpu.HBM if by_row else pltpu.VMEM)((8, 2, 8, 64, 128), BF16),
         scratch_shapes=[
-            pltpu.VMEM((2, 8, 8, 64, 128), BF16),
-            pltpu.SemaphoreType.DMA((4, 2)),
+            pltpu.VMEM((8, 2, 8, 64, 128), BF16),
+            pltpu.SemaphoreType.DMA((4,)),
         ]
         if by_row
         else [],
@@ -226,6 +226,13 @@
     )
 
 
+def by_source(weights):
+    rows = weights.astype(F32)
+    return jnp.concatenate(
+        [rows[p * 64 + r * 8 : p * 64 + r * 8 + 8] for r in range(8) for p in range(2)], 0
+    ).astype(BF16)
+
+
 def middle_kernel(
     rep_ref, hidden_ref, state_ref, gate_ref, mine_ref, other_ref, w_gate_ref, new_ref,
     new_gate_ref, out_ref, spread, sides, old_state, old_gate, load_sems,
@@ -245,7 +252,7 @@
         )
     for load in loads[0] + loads[1]:
         load.start()
-    w_out = both_halves(rep_ref, mine_ref[256:320], other_ref[256:320])
+    w_out = by_source(both_halves(rep_ref, mine_ref[256:320], other_ref[256:320]))
     weights = both_halves(rep_ref, mine_ref[:256], other_ref[:256])
     for first in range(0, 64, ROWS):
         where = slice(first * 128, (first + ROWS) * 128)
@@ -378,7 +385,7 @@
     pair, w_left, w_left_gate, w_right, w_right_gate, w_gate, w_out, w_trans_in, w_trans_out
 ):
     rep = lax.axis_index("rep").astype(jnp.int32).reshape(1)
-    everywhere = ("rep", "row", "col")
+    everywhere = ("row", "rep", "col")
     projections = [
         w.transpose(0, 2, 1) for w in (w_left, w_left_gate, w_right, w_right_gate)
     ]
@@ -408,7 +415,7 @@
 
     state, gate, sides = middle(rep, near(hidden), far(state), far(gate), mine, other, gates[1])
     received = exchange(sides, everywhere)
-    hidden = exchange(product(near(received.reshape(2, 8, 8, 2, 64, 128)), False), everywhere)
+    hidden = exchange(product(near(received.reshape(8, 2, 8, 2, 64, 128)), False), everywhere)
     return finish(rep, near(hidden), state, gate, mine, other, w_in, w_down)
 
 

time: 222 us -> 220 us (level)
  no operation moved by 1% of the time
where the time goes in v5:
time: 220 us; the launch traced here: 219 us
  blocking collectives  154 us (70%)
  Pallas kernels  33.4 us (15%)
  waiting for transfers between devices  20.4 us (9%)
  starting transfers between devices  8.95 us (4%)
  local copies, waits for them, and re-layouts  2.67 us (1%)
    all_to_all x3, blocking collectives, exchange(): return lax.all_to_all(values, axes, split_axis=0, concat_axis=0, tiled=True)  154 us
    ppermute x1, waiting for transfers between devices, on_device(): other = lax.ppermute(mine, 'rep', [(0, 1), (1, 0)])  17.7 us
    pallas_call x1, Pallas kernels, finish(): pl.pallas_call(finish_kernel, name='finish', in_specs=[SMEM] + [VMEM] * 7...  10.4 us
    pallas_call x1, Pallas kernels, middle(): pl.pallas_call(middle_kernel, name='middle', in_specs=[SMEM, VMEM, ANY, A...  7.47 us
    pallas_call x1, Pallas kernels, front(): pl.pallas_call(front_kernel, name='front', in_specs=[ANY] * 5, out_specs=...  6.08 us
    all_to_all x1, starting transfers between devices, exchange(): return lax.all_to_all(values, axes, split_axis=0, concat_axis=0, tiled=True)  5.8 us
    pallas_call x2, Pallas kernels, product(): pl.pallas_call(functools.partial(product_kernel, by_row=by_row), name='pr...  5.55 us
  transfers between devices with their start and end apart: 2, of which 2 were waited for; matrix products, arithmetic and copies ran while one was open for 0% of the time, Pallas kernels for 2%

profile of v5, /device:TPU:1, one launch (start us, length us, event | category | flops | bytes accessed | tf_op | source)
XLA Modules:
  0.0 219.3 jit_solution(13244101582593628656)
XLA Ops:
  0.0 6.1 %front.1 = bf16[64,2,128,128]{3,2,1,0:T(8,128)(2,1)S(1)} custom-call(bf16[128,128,128]{2,1,0:T(8,128)(2,1)} %pair_ref.2, bf16[2,64,128]{2,1,0:T(8,128)(2,1)} %bitcast.35, bf16[2,64,128]{2,1,0:T(8,128)(2,1)} %bitcast.37, bf16[2,64,128]{2,1,0:T(8,128)(2,1)} %bitcast.39, bf16[2,64,128]{2,1,0:T(8,128)(2,1)} %bitcast.41), custom_call_target="tpu_custom_call" | custom-call | flops 1610612736 | bytes 12582912 | tf_op jit(solution)/shard_map/front/pallas_call | solution.py:94
  6.1 61.7 %all_to_all.20 = bf16[64,2,128,128]{3,2,1,0:T(8,128)(2,1)S(1)} all-to-all(bf16[64,2,128,128]{3,2,1,0:T(8,128)(2,1)S(1)} %front.1), channel_id=1, replica_groups=mesh['row'=8,'col'=8,'rep'=2] {'row','col'}, dimensions={0} | all-to-all | bytes 8388608 | tf_op jit(solution)/shard_map/all_to_all | solution.py:373
  67.8 3.2 %product_out.1 = bf16[8,2,8,64,128]{4,3,2,1,0:T(8,128)(2,1)} custom-call(bf16[8,8,2,128,128]{4,3,2,1,0:T(8,128)(2,1)S(1)} %bitcast.29), custom_call_target="tpu_custom_call" | custom-call | flops 2147483648 | bytes 6291456 | tf_op jit(solution)/shard_map/product_out/pallas_call | solution.py:186
  71.0 0.0 copy-start.7
  71.0 0.0 copy-start.3
  71.0 0.0 copy-start.4
  71.0 0.0 copy-start.5
  71.0 0.0 copy-start.6
  71.0 0.0 copy-start.8
  71.0 0.0 copy-start.2
  71.0 0.0 copy-start.1
  71.1 5.8 %all-to-all-start.1 = ((bf16[128,64,128]{2,1,0:T(8,128)(2,1)}), bf16[128,64,128]{2,1,0:T(8,128)(2,1)S(1)}, u32[]{:S(2)}, u32[]{:S(2)}) async-start(bf16[128,64,128]{2,1,0:T(8,128)(2,1)} %bitcast.34), calls=%async_computation.1 | async-start | bytes 4194304 | tf_op jit(solution)/shard_map/all_to_all | solution.py:373
  76.9 0.0 copy-done.7
  76.9 0.1 copy.10
  77.0 0.0 copy-done.3
  77.0 0.0 copy-done.4
  77.0 0.0 copy-done.5
  77.1 0.0 copy-done.6
  77.1 0.0 copy-done.8
  77.1 3.2 %collective-permute-start = (bf16[384,128]{1,0:T(8,128)(2,1)S(1)}, bf16[384,128]{1,0:T(8,128)(2,1)S(1)}, u32[]{:S(2)}, u32[]{:S(2)}) collective-permute-start(bf16[384,128]{1,0:T(8,128)(2,1)S(1)} %bitcast_dynamic-update-slice_fusion.mine_ref), channel_id=1, source_target_pairs={{0,1},{1,0},{2,3},{3,2},{4,5},{5,4},{6,7},{7,6},{8,9},{9,8},{10,11... | collective-permute-start | bytes 294920 | tf_op jit(solution)/shard_map/ppermute | solution.py:407
  80.3 0.0 copy-done.2
  80.3 0.1 copy.12
  80.4 0.0 copy-done.1
  80.5 0.2 copy.11
  80.6 0.0 copy-start
  80.6 2.2 copy-done
  82.8 3.9 %turn.1 = (bf16[128,8192]{1,0:T(8,128)(2,1)}, bf16[128,8192]{1,0:T(8,128)(2,1)}) custom-call(s32[1]{0:T(128)} %bitcast.4.rep_ref, bf16[128,128,128]{2,1,0:T(8,128)(2,1)S(1)} %copy-done, bf16[128,128]{1,0:T(8,128)(2,1)S(1)} %slice_bitcast_fusion.w_ref), custom_call_target="tpu_custom_call" | custom-call | flops 536870912 | bytes 6291456 | tf_op jit(solution)/shard_map/turn/pallas_call | solution.py:129
  86.7 17.7 %collective-permute-done.other_ref = bf16[384,128]{1,0:T(8,128)(2,1)S(1)} collective-permute-done((bf16[384,128]{1,0:T(8,128)(2,1)S(1)}, bf16[384,128]{1,0:T(8,128)(2,1)S(1)}, u32[]{:S(2)}, u32[]{:S(2)}) %collective-permute-start) | collective-permute-done | bytes 98336 | tf_op jit(solution)/shard_map/ppermute | solution.py:407
  104.4 2.7 %all-to-all-done.1.hidden_ref = bf16[128,64,128]{2,1,0:T(8,128)(2,1)S(1)} async-done(((bf16[128,64,128]{2,1,0:T(8,128)(2,1)}), bf16[128,64,128]{2,1,0:T(8,128)(2,1)S(1)}, u32[]{:S(2)}, u32[]{:S(2)}) %all-to-all-start.1) | async-done | bytes 2097184 | tf_op jit(solution)/shard_map/all_to_all | solution.py:373
  107.1 7.5 %middle.1 = (bf16[128,8192]{1,0:T(8,128)(2,1)S(1)}, bf16[128,8192]{1,0:T(8,128)(2,1)S(1)}, bf16[128,2,64,128]{3,2,1,0:T(8,128)(2,1)S(1)}) custom-call(s32[1]{0:T(128)} %bitcast.4.rep_ref, bf16[128,64,128]{2,1,0:T(8,128)(2,1)S(1)} %all-to-all-done.1.hidden_ref, bf16[128,8192]{1,0:T(8,128)(2,1)} %get-tuple-element.45.state_ref, ...), custom_call_target="tpu_custom_call" | custom-call | flops 1342177280 | bytes 14680064 | tf_op jit(solution)/shard_map/middle/pallas_call | solution.py:290
  114.6 58.1 %all_to_all.21 = bf16[128,2,64,128]{3,2,1,0:T(8,128)(2,1)S(1)} all-to-all(bf16[128,2,64,128]{3,2,1,0:T(8,128)(2,1)S(1)} %get-tuple-element.50), channel_id=1, replica_groups=mesh['row'=8,'col'=8,'rep'=2] {'row','rep','col'}, dimensions={0} | all-to-all | bytes 8388608 | tf_op jit(solution)/shard_map/all_to_all | solution.py:373
  172.6 2.4 %product_in.1 = bf16[8,2,8,64,128]{4,3,2,1,0:T(8,128)(2,1)S(1)} custom-call(bf16[8,2,8,2,64,128]{5,4,3,2,1,0:T(8,128)(2,1)S(1)} %bitcast.30), custom_call_target="tpu_custom_call" | custom-call | flops 2147483648 | bytes 6291456 | tf_op jit(solution)/shard_map/product_in/pallas_call | solution.py:186
  175.0 33.8 %all_to_all.22.hidden_ref = bf16[128,64,128]{2,1,0:T(8,128)(2,1)S(1)} all-to-all(bf16[128,64,128]{2,1,0:T(8,128)(2,1)S(1)} %bitcast.31), channel_id=1, replica_groups=mesh['row'=8,'col'=8,'rep'=2] {'row','rep','col'}, dimensions={0} | all-to-all | bytes 4194304 | tf_op jit(solution)/shard_map/all_to_all | solution.py:373
  208.8 10.4 %finish.1 = bf16[128,64,128]{2,1,0:T(8,128)(2,1)} custom-call(s32[1]{0:T(128)} %bitcast.4.rep_ref, bf16[128,64,128]{2,1,0:T(8,128)(2,1)S(1)} %all_to_all.22.hidden_ref, bf16[128,8192]{1,0:T(8,128)(2,1)S(1)} %get-tuple-element.51.state_ref, bf16[128,8192]{1,0:T(8,128)(2,1)S(1)} %get-tuple-element.52.gate_ref, ...), custom_call_target="tpu_custom_call" | custom-call | flops 3489660928 | bytes 10485760 | tf_op jit(solution)/shard_map/finish/pallas_call | solution.py:353
  (9 shorter events, 0.1 us)
Async XLA Ops:
  71.0 5.9 %copy-start.7 = (bf16[2,128,128]{2,1,0:T(8,128)(2,1)S(1)}, bf16[2,128,128]{2,1,0:T(8,128)(2,1)}, u32[]{:S(2)}) copy-start(bf16[2,128,128]{2,1,0:T(8,128)(2,1)} %param.14) | copy-start | bytes 196612
  71.0 6.0 %copy-start.3 = (bf16[2,128,64]{1,2,0:T(8,128)(2,1)S(1)}, bf16[2,128,64]{1,2,0:T(8,128)(2,1)}, u32[]{:S(2)}) copy-start(bf16[2,128,64]{1,2,0:T(8,128)(2,1)} %param.10) | copy-start | bytes 98308
  71.0 6.0 %copy-start.4 = (bf16[2,128,64]{1,2,0:T(8,128)(2,1)S(1)}, bf16[2,128,64]{1,2,0:T(8,128)(2,1)}, u32[]{:S(2)}) copy-start(bf16[2,128,64]{1,2,0:T(8,128)(2,1)} %param.11) | copy-start | bytes 98308
  71.0 6.1 %copy-start.5 = (bf16[2,128,64]{1,2,0:T(8,128)(2,1)S(1)}, bf16[2,128,64]{1,2,0:T(8,128)(2,1)}, u32[]{:S(2)}) copy-start(bf16[2,128,64]{1,2,0:T(8,128)(2,1)} %param.12) | copy-start | bytes 98308
  71.0 6.1 %copy-start.6 = (bf16[2,128,64]{1,2,0:T(8,128)(2,1)S(1)}, bf16[2,128,64]{1,2,0:T(8,128)(2,1)}, u32[]{:S(2)}) copy-start(bf16[2,128,64]{1,2,0:T(8,128)(2,1)} %param.13) | copy-start | bytes 98308
  71.0 6.1 %copy-start.8 = (bf16[2,64,128]{2,1,0:T(8,128)(2,1)S(1)}, bf16[2,64,128]{2,1,0:T(8,128)(2,1)}, u32[]{:S(2)}) copy-start(bf16[2,64,128]{2,1,0:T(8,128)(2,1)} %param.15) | copy-start | bytes 98308
  71.0 9.3 %copy-start.2 = (bf16[512,128]{1,0:T(8,128)(2,1)S(1)}, bf16[512,128]{1,0:T(8,128)(2,1)}, u32[]{:S(2)}) copy-start(bf16[512,128]{1,0:T(8,128)(2,1)} %param.17) | copy-start | bytes 393220
  71.0 9.4 %copy-start.1 = (bf16[128,1024]{1,0:T(8,128)(2,1)S(1)}, bf16[128,1024]{1,0:T(8,128)(2,1)}, u32[]{:S(2)}) copy-start(bf16[128,1024]{1,0:T(8,128)(2,1)} %param.16) | copy-start | bytes 786436
  71.1 36.0 %all-to-all-start.1 = ((bf16[128,64,128]{2,1,0:T(8,128)(2,1)}), bf16[128,64,128]{2,1,0:T(8,128)(2,1)S(1)}, u32[]{:S(2)}, u32[]{:S(2)}) async-start(bf16[128,64,128]{2,1,0:T(8,128)(2,1)} %bitcast.34), calls=%async_computation.1 | async-start | bytes 4194304 | tf_op jit(solution)/shard_map/all_to_all | solution.py:373
  77.1 27.3 %collective-permute-start = (bf16[384,128]{1,0:T(8,128)(2,1)S(1)}, bf16[384,128]{1,0:T(8,128)(2,1)S(1)}, u32[]{:S(2)}, u32[]{:S(2)}) collective-permute-start(bf16[384,128]{1,0:T(8,128)(2,1)S(1)} %bitcast_dynamic-update-slice_fusion.mine_ref), channel_id=1, source_target_pairs={{0,1},{1,0},{2,3},{3,2},{4,5},{5,4},{6,7},{7,6},{8,9},{9,8},{10,11... | collective-permute-start | bytes 294920 | tf_op jit(solution)/shard_map/ppermute | solution.py:407
  80.6 2.2 %copy-start = (bf16[128,128,128]{2,1,0:T(8,128)(2,1)S(1)}, bf16[128,128,128]{2,1,0:T(8,128)(2,1)}, u32[]{:S(2)}) copy-start(bf16[128,128,128]{2,1,0:T(8,128)(2,1)} %pair_ref.2) | copy-start | bytes 12582916

commit v6 on v5

--- a/solution.py
+++ b/solution.py
@@ -100,7 +100,7 @@
         scratch_shapes=[
             pltpu.VMEM((128, 128, 128), BF16),
             pltpu.VMEM((256, 128), BF16),
-            pltpu.VMEM((2, 64 * FRONT_PITCH, 128), F32),
+            pltpu.VMEM((2, 65 * FRONT_PITCH, 128), F32),
             pltpu.SemaphoreType.DMA((128 // FRONT_ROWS,)),
             pltpu.SemaphoreType.DMA((4,)),
         ],
@@ -137,7 +137,7 @@
                 pl.BlockSpec((128, 128), lambda s, rep: (0, 0)),
             ],
             out_specs=[pl.BlockSpec((128, FRONT_ROWS * 128), lambda s, rep: (0, s))] * 2,
-            scratch_shapes=[pltpu.VMEM((128 * FRONT_PITCH, 128), F32)],
+            scratch_shapes=[pltpu.VMEM((129 * FRONT_PITCH, 128), F32)],
         ),
         out_shape=[pltpu.HBM((128, 8192), BF16)] * 2,
         compiler_params=params(36),
@@ -298,8 +298,8 @@
             pltpu.VMEM((128, 2, 64, 128), BF16),
         ],
         scratch_shapes=[
-            pltpu.VMEM((128 * PITCH, 128), F32),
-            pltpu.VMEM((2, 128 * PITCH, 128), F32),
+            pltpu.VMEM((129 * PITCH, 128), F32),
+            pltpu.VMEM((2, 129 * PITCH, 128), F32),
             pltpu.VMEM((128, 8192), BF16),
             pltpu.VMEM((128, 8192), BF16),
             pltpu.SemaphoreType.DMA((2, 64 // ROWS)),
@@ -357,10 +357,10 @@
         out_specs=ANY,
         out_shape=pltpu.HBM((128, 64, 128), BF16),
         scratch_shapes=[
-            pltpu.VMEM((128 * PITCH, 128), F32),
+            pltpu.VMEM((129 * PITCH, 128), F32),
             pltpu.VMEM((128, ROWS * 128), F32),
             pltpu.VMEM((128, ROWS * 128), BF16),
-            pltpu.VMEM((128 * PITCH, 128), F32),
+            pltpu.VMEM((129 * PITCH, 128), F32),
             pltpu.VMEM((128, 64, 128), BF16),
             pltpu.SemaphoreType.DMA((64 // ROWS,)),
         ],

time: 220 us -> 220 us (level)
  no operation moved by 1% of the time
where the time goes in v6:
time: 220 us; the launch traced here: 219 us
  blocking collectives  154 us (70%)
  Pallas kernels  33.4 us (15%)
  waiting for transfers between devices  20.4 us (9%)
  starting transfers between devices  8.94 us (4%)
  local copies, waits for them, and re-layouts  2.67 us (1%)
    all_to_all x3, blocking collectives, exchange(): return lax.all_to_all(values, axes, split_axis=0, concat_axis=0, tiled=True)  154 us
    ppermute x1, waiting for transfers between devices, on_device(): other = lax.ppermute(mine, 'rep', [(0, 1), (1, 0)])  17.7 us
    pallas_call x1, Pallas kernels, finish(): pl.pallas_call(finish_kernel, name='finish', in_specs=[SMEM] + [VMEM] * 7...  10.4 us
    pallas_call x1, Pallas kernels, middle(): pl.pallas_call(middle_kernel, name='middle', in_specs=[SMEM, VMEM, ANY, A...  7.48 us
    pallas_call x1, Pallas kernels, front(): pl.pallas_call(front_kernel, name='front', in_specs=[ANY] * 5, out_specs=...  6.08 us
    all_to_all x1, starting transfers between devices, exchange(): return lax.all_to_all(values, axes, split_axis=0, concat_axis=0, tiled=True)  5.79 us
    pallas_call x2, Pallas kernels, product(): pl.pallas_call(functools.partial(product_kernel, by_row=by_row), name='pr...  5.55 us
  transfers between devices with their start and end apart: 2, of which 2 were waited for; matrix products, arithmetic and copies ran while one was open for 0% of the time, Pallas kernels for 2%

profile of v6, /device:TPU:1, one launch (start us, length us, event | category | flops | bytes accessed | tf_op | source)
XLA Modules:
  0.0 219.4 jit_solution(8559352211723060986)
XLA Ops:
  0.0 6.1 %front.1 = bf16[64,2,128,128]{3,2,1,0:T(8,128)(2,1)S(1)} custom-call(bf16[128,128,128]{2,1,0:T(8,128)(2,1)} %pair_ref.2, bf16[2,64,128]{2,1,0:T(8,128)(2,1)} %bitcast.35, bf16[2,64,128]{2,1,0:T(8,128)(2,1)} %bitcast.37, bf16[2,64,128]{2,1,0:T(8,128)(2,1)} %bitcast.39, bf16[2,64,128]{2,1,0:T(8,128)(2,1)} %bitcast.41), custom_call_target="tpu_custom_call" | custom-call | flops 1610612736 | bytes 12582912 | tf_op jit(solution)/shard_map/front/pallas_call | solution.py:94
  6.1 61.7 %all_to_all.20 = bf16[64,2,128,128]{3,2,1,0:T(8,128)(2,1)S(1)} all-to-all(bf16[64,2,128,128]{3,2,1,0:T(8,128)(2,1)S(1)} %front.1), channel_id=1, replica_groups=mesh['row'=8,'col'=8,'rep'=2] {'row','col'}, dimensions={0} | all-to-all | bytes 8388608 | tf_op jit(solution)/shard_map/all_to_all | solution.py:373
  67.8 3.2 %product_out.1 = bf16[8,2,8,64,128]{4,3,2,1,0:T(8,128)(2,1)} custom-call(bf16[8,8,2,128,128]{4,3,2,1,0:T(8,128)(2,1)S(1)} %bitcast.29), custom_call_target="tpu_custom_call" | custom-call | flops 2147483648 | bytes 6291456 | tf_op jit(solution)/shard_map/product_out/pallas_call | solution.py:186
  71.0 0.0 copy-start.7
  71.0 0.0 copy-start.3
  71.0 0.0 copy-start.4
  71.0 0.0 copy-start.5
  71.0 0.0 copy-start.6
  71.0 0.0 copy-start.8
  71.0 0.0 copy-start.2
  71.0 0.0 copy-start.1
  71.1 5.8 %all-to-all-start.1 = ((bf16[128,64,128]{2,1,0:T(8,128)(2,1)}), bf16[128,64,128]{2,1,0:T(8,128)(2,1)S(1)}, u32[]{:S(2)}, u32[]{:S(2)}) async-start(bf16[128,64,128]{2,1,0:T(8,128)(2,1)} %bitcast.34), calls=%async_computation.1 | async-start | bytes 4194304 | tf_op jit(solution)/shard_map/all_to_all | solution.py:373
  76.9 0.0 copy-done.7
  76.9 0.1 copy.10
  77.0 0.0 copy-done.3
  77.0 0.0 copy-done.4
  77.0 0.0 copy-done.5
  77.1 0.0 copy-done.6
  77.1 0.0 copy-done.8
  77.1 3.2 %collective-permute-start = (bf16[384,128]{1,0:T(8,128)(2,1)S(1)}, bf16[384,128]{1,0:T(8,128)(2,1)S(1)}, u32[]{:S(2)}, u32[]{:S(2)}) collective-permute-start(bf16[384,128]{1,0:T(8,128)(2,1)S(1)} %bitcast_dynamic-update-slice_fusion.mine_ref), channel_id=1, source_target_pairs={{0,1},{1,0},{2,3},{3,2},{4,5},{5,4},{6,7},{7,6},{8,9},{9,8},{10,11... | collective-permute-start | bytes 294920 | tf_op jit(solution)/shard_map/ppermute | solution.py:407
  80.3 0.0 copy-done.2
  80.3 0.1 copy.12
  80.4 0.0 copy-done.1
  80.5 0.2 copy.11
  80.6 0.0 copy-start
  80.6 2.2 copy-done
  82.8 3.9 %turn.1 = (bf16[128,8192]{1,0:T(8,128)(2,1)}, bf16[128,8192]{1,0:T(8,128)(2,1)}) custom-call(s32[1]{0:T(128)} %bitcast.4.rep_ref, bf16[128,128,128]{2,1,0:T(8,128)(2,1)S(1)} %copy-done, bf16[128,128]{1,0:T(8,128)(2,1)S(1)} %slice_bitcast_fusion.w_ref), custom_call_target="tpu_custom_call" | custom-call | flops 536870912 | bytes 6291456 | tf_op jit(solution)/shard_map/turn/pallas_call | solution.py:129
  86.7 17.7 %collective-permute-done.other_ref = bf16[384,128]{1,0:T(8,128)(2,1)S(1)} collective-permute-done((bf16[384,128]{1,0:T(8,128)(2,1)S(1)}, bf16[384,128]{1,0:T(8,128)(2,1)S(1)}, u32[]{:S(2)}, u32[]{:S(2)}) %collective-permute-start) | collective-permute-done | bytes 98336 | tf_op jit(solution)/shard_map/ppermute | solution.py:407
  104.4 2.7 %all-to-all-done.1.hidden_ref = bf16[128,64,128]{2,1,0:T(8,128)(2,1)S(1)} async-done(((bf16[128,64,128]{2,1,0:T(8,128)(2,1)}), bf16[128,64,128]{2,1,0:T(8,128)(2,1)S(1)}, u32[]{:S(2)}, u32[]{:S(2)}) %all-to-all-start.1) | async-done | bytes 2097184 | tf_op jit(solution)/shard_map/all_to_all | solution.py:373
  107.1 7.5 %middle.1 = (bf16[128,8192]{1,0:T(8,128)(2,1)S(1)}, bf16[128,8192]{1,0:T(8,128)(2,1)S(1)}, bf16[128,2,64,128]{3,2,1,0:T(8,128)(2,1)S(1)}) custom-call(s32[1]{0:T(128)} %bitcast.4.rep_ref, bf16[128,64,128]{2,1,0:T(8,128)(2,1)S(1)} %all-to-all-done.1.hidden_ref, bf16[128,8192]{1,0:T(8,128)(2,1)} %get-tuple-element.45.state_ref, ...), custom_call_target="tpu_custom_call" | custom-call | flops 1342177280 | bytes 14680064 | tf_op jit(solution)/shard_map/middle/pallas_call | solution.py:290
  114.6 58.1 %all_to_all.21 = bf16[128,2,64,128]{3,2,1,0:T(8,128)(2,1)S(1)} all-to-all(bf16[128,2,64,128]{3,2,1,0:T(8,128)(2,1)S(1)} %get-tuple-element.50), channel_id=1, replica_groups=mesh['row'=8,'col'=8,'rep'=2] {'row','rep','col'}, dimensions={0} | all-to-all | bytes 8388608 | tf_op jit(solution)/shard_map/all_to_all | solution.py:373
  172.7 2.4 %product_in.1 = bf16[8,2,8,64,128]{4,3,2,1,0:T(8,128)(2,1)S(1)} custom-call(bf16[8,2,8,2,64,128]{5,4,3,2,1,0:T(8,128)(2,1)S(1)} %bitcast.30), custom_call_target="tpu_custom_call" | custom-call | flops 2147483648 | bytes 6291456 | tf_op jit(solution)/shard_map/product_in/pallas_call | solution.py:186
  175.0 33.8 %all_to_all.22.hidden_ref = bf16[128,64,128]{2,1,0:T(8,128)(2,1)S(1)} all-to-all(bf16[128,64,128]{2,1,0:T(8,128)(2,1)S(1)} %bitcast.31), channel_id=1, replica_groups=mesh['row'=8,'col'=8,'rep'=2] {'row','rep','col'}, dimensions={0} | all-to-all | bytes 4194304 | tf_op jit(solution)/shard_map/all_to_all | solution.py:373
  208.8 10.4 %finish.1 = bf16[128,64,128]{2,1,0:T(8,128)(2,1)} custom-call(s32[1]{0:T(128)} %bitcast.4.rep_ref, bf16[128,64,128]{2,1,0:T(8,128)(2,1)S(1)} %all_to_all.22.hidden_ref, bf16[128,8192]{1,0:T(8,128)(2,1)S(1)} %get-tuple-element.51.state_ref, bf16[128,8192]{1,0:T(8,128)(2,1)S(1)} %get-tuple-element.52.gate_ref, ...), custom_call_target="tpu_custom_call" | custom-call | flops 3489660928 | bytes 10485760 | tf_op jit(solution)/shard_map/finish/pallas_call | solution.py:353
  (9 shorter events, 0.1 us)
Async XLA Ops:
  71.0 5.9 %copy-start.7 = (bf16[2,128,128]{2,1,0:T(8,128)(2,1)S(1)}, bf16[2,128,128]{2,1,0:T(8,128)(2,1)}, u32[]{:S(2)}) copy-start(bf16[2,128,128]{2,1,0:T(8,128)(2,1)} %param.14) | copy-start | bytes 196612
  71.0 6.0 %copy-start.3 = (bf16[2,128,64]{1,2,0:T(8,128)(2,1)S(1)}, bf16[2,128,64]{1,2,0:T(8,128)(2,1)}, u32[]{:S(2)}) copy-start(bf16[2,128,64]{1,2,0:T(8,128)(2,1)} %param.10) | copy-start | bytes 98308
  71.0 6.0 %copy-start.4 = (bf16[2,128,64]{1,2,0:T(8,128)(2,1)S(1)}, bf16[2,128,64]{1,2,0:T(8,128)(2,1)}, u32[]{:S(2)}) copy-start(bf16[2,128,64]{1,2,0:T(8,128)(2,1)} %param.11) | copy-start | bytes 98308
  71.0 6.1 %copy-start.5 = (bf16[2,128,64]{1,2,0:T(8,128)(2,1)S(1)}, bf16[2,128,64]{1,2,0:T(8,128)(2,1)}, u32[]{:S(2)}) copy-start(bf16[2,128,64]{1,2,0:T(8,128)(2,1)} %param.12) | copy-start | bytes 98308
  71.0 6.1 %copy-start.6 = (bf16[2,128,64]{1,2,0:T(8,128)(2,1)S(1)}, bf16[2,128,64]{1,2,0:T(8,128)(2,1)}, u32[]{:S(2)}) copy-start(bf16[2,128,64]{1,2,0:T(8,128)(2,1)} %param.13) | copy-start | bytes 98308
  71.0 6.1 %copy-start.8 = (bf16[2,64,128]{2,1,0:T(8,128)(2,1)S(1)}, bf16[2,64,128]{2,1,0:T(8,128)(2,1)}, u32[]{:S(2)}) copy-start(bf16[2,64,128]{2,1,0:T(8,128)(2,1)} %param.15) | copy-start | bytes 98308
  71.0 9.3 %copy-start.2 = (bf16[512,128]{1,0:T(8,128)(2,1)S(1)}, bf16[512,128]{1,0:T(8,128)(2,1)}, u32[]{:S(2)}) copy-start(bf16[512,128]{1,0:T(8,128)(2,1)} %param.17) | copy-start | bytes 393220
  71.0 9.4 %copy-start.1 = (bf16[128,1024]{1,0:T(8,128)(2,1)S(1)}, bf16[128,1024]{1,0:T(8,128)(2,1)}, u32[]{:S(2)}) copy-start(bf16[128,1024]{1,0:T(8,128)(2,1)} %param.16) | copy-start | bytes 786436
  71.1 36.0 %all-to-all-start.1 = ((bf16[128,64,128]{2,1,0:T(8,128)(2,1)}), bf16[128,64,128]{2,1,0:T(8,128)(2,1)S(1)}, u32[]{:S(2)}, u32[]{:S(2)}) async-start(bf16[128,64,128]{2,1,0:T(8,128)(2,1)} %bitcast.34), calls=%async_computation.1 | async-start | bytes 4194304 | tf_op jit(solution)/shard_map/all_to_all | solution.py:373
  77.1 27.3 %collective-permute-start = (bf16[384,128]{1,0:T(8,128)(2,1)S(1)}, bf16[384,128]{1,0:T(8,128)(2,1)S(1)}, u32[]{:S(2)}, u32[]{:S(2)}) collective-permute-start(bf16[384,128]{1,0:T(8,128)(2,1)S(1)} %bitcast_dynamic-update-slice_fusion.mine_ref), channel_id=1, source_target_pairs={{0,1},{1,0},{2,3},{3,2},{4,5},{5,4},{6,7},{7,6},{8,9},{9,8},{10,11... | collective-permute-start | bytes 294920 | tf_op jit(solution)/shard_map/ppermute | solution.py:407
  80.6 2.2 %copy-start = (bf16[128,128,128]{2,1,0:T(8,128)(2,1)S(1)}, bf16[128,128,128]{2,1,0:T(8,128)(2,1)}, u32[]{:S(2)}) copy-start(bf16[128,128,128]{2,1,0:T(8,128)(2,1)} %pair_ref.2) | copy-start | bytes 12582916

commit v7 on v6

--- a/solution.py
+++ b/solution.py
@@ -327,9 +327,9 @@
         for start in range(0, ROWS, group):
             part = slice(start * 128, (start + group) * 128)
             normed = normed_scr[:, part]
-            half_gate = dot(w_half_gate, normed)
-            linear = dot(w_in_ref[512:], normed)
-            active = (gated(half_gate, half_gate) * linear).astype(BF16)
+            half_gate = dot(w_half_gate, normed).astype(BF16)
+            linear = dot(w_in_ref[512:], normed).astype(BF16)
+            active = gated(half_gate, half_gate) * linear
             updated = state_scr[:, part] + dot(w_down_ref[...], active)
             for row in range(group):
                 turned[pl.ds(start + row, 128, stride=PITCH), :] = updated[

time: 220 us -> 219 us (level)
  no operation moved by 1% of the time
where the time goes in v7:
time: 219 us
  blocking collectives  154 us (70%)
  Pallas kernels  32.9 us (15%)
  waiting for transfers between devices  20.4 us (9%)
  starting transfers between devices  8.94 us (4%)
  local copies, waits for them, and re-layouts  2.67 us (1%)
    all_to_all x3, blocking collectives, exchange(): return lax.all_to_all(values, axes, split_axis=0, concat_axis=0, tiled=True)  154 us
    ppermute x1, waiting for transfers between devices, on_device(): other = lax.ppermute(mine, 'rep', [(0, 1), (1, 0)])  17.7 us
    pallas_call x1, Pallas kernels, finish(): pl.pallas_call(finish_kernel, name='finish', in_specs=[SMEM] + [VMEM] * 7...  9.84 us
    pallas_call x1, Pallas kernels, middle(): pl.pallas_call(middle_kernel, name='middle', in_specs=[SMEM, VMEM, ANY, A...  7.48 us
    pallas_call x1, Pallas kernels, front(): pl.pallas_call(front_kernel, name='front', in_specs=[ANY] * 5, out_specs=...  6.08 us
    all_to_all x1, starting transfers between devices, exchange(): return lax.all_to_all(values, axes, split_axis=0, concat_axis=0, tiled=True)  5.79 us
    pallas_call x2, Pallas kernels, product(): pl.pallas_call(functools.partial(product_kernel, by_row=by_row), name='pr...  5.55 us
  transfers between devices with their start and end apart: 2, of which 2 were waited for; matrix products, arithmetic and copies ran while one was open for 0% of the time, Pallas kernels for 2%

profile of v7, /device:TPU:1, one launch (start us, length us, event | category | flops | bytes accessed | tf_op | source)
XLA Modules:
  0.0 218.8 jit_solution(8266018182615546124)
XLA Ops:
  0.0 6.1 %front.1 = bf16[64,2,128,128]{3,2,1,0:T(8,128)(2,1)S(1)} custom-call(bf16[128,128,128]{2,1,0:T(8,128)(2,1)} %pair_ref.2, bf16[2,64,128]{2,1,0:T(8,128)(2,1)} %bitcast.35, bf16[2,64,128]{2,1,0:T(8,128)(2,1)} %bitcast.37, bf16[2,64,128]{2,1,0:T(8,128)(2,1)} %bitcast.39, bf16[2,64,128]{2,1,0:T(8,128)(2,1)} %bitcast.41), custom_call_target="tpu_custom_call" | custom-call | flops 1610612736 | bytes 12582912 | tf_op jit(solution)/shard_map/front/pallas_call | solution.py:94
  6.1 61.7 %all_to_all.20 = bf16[64,2,128,128]{3,2,1,0:T(8,128)(2,1)S(1)} all-to-all(bf16[64,2,128,128]{3,2,1,0:T(8,128)(2,1)S(1)} %front.1), channel_id=1, replica_groups=mesh['row'=8,'col'=8,'rep'=2] {'row','col'}, dimensions={0} | all-to-all | bytes 8388608 | tf_op jit(solution)/shard_map/all_to_all | solution.py:373
  67.8 3.2 %product_out.1 = bf16[8,2,8,64,128]{4,3,2,1,0:T(8,128)(2,1)} custom-call(bf16[8,8,2,128,128]{4,3,2,1,0:T(8,128)(2,1)S(1)} %bitcast.29), custom_call_target="tpu_custom_call" | custom-call | flops 2147483648 | bytes 6291456 | tf_op jit(solution)/shard_map/product_out/pallas_call | solution.py:186
  71.0 0.0 copy-start.7
  71.0 0.0 copy-start.3
  71.0 0.0 copy-start.4
  71.0 0.0 copy-start.5
  71.0 0.0 copy-start.6
  71.0 0.0 copy-start.8
  71.0 0.0 copy-start.2
  71.0 0.0 copy-start.1
  71.1 5.8 %all-to-all-start.1 = ((bf16[128,64,128]{2,1,0:T(8,128)(2,1)}), bf16[128,64,128]{2,1,0:T(8,128)(2,1)S(1)}, u32[]{:S(2)}, u32[]{:S(2)}) async-start(bf16[128,64,128]{2,1,0:T(8,128)(2,1)} %bitcast.34), calls=%async_computation.1 | async-start | bytes 4194304 | tf_op jit(solution)/shard_map/all_to_all | solution.py:373
  76.9 0.0 copy-done.7
  76.9 0.1 copy.10
  77.0 0.0 copy-done.3
  77.0 0.0 copy-done.4
  77.0 0.0 copy-done.5
  77.1 0.0 copy-done.6
  77.1 0.0 copy-done.8
  77.1 3.2 %collective-permute-start = (bf16[384,128]{1,0:T(8,128)(2,1)S(1)}, bf16[384,128]{1,0:T(8,128)(2,1)S(1)}, u32[]{:S(2)}, u32[]{:S(2)}) collective-permute-start(bf16[384,128]{1,0:T(8,128)(2,1)S(1)} %bitcast_dynamic-update-slice_fusion.mine_ref), channel_id=1, source_target_pairs={{0,1},{1,0},{2,3},{3,2},{4,5},{5,4},{6,7},{7,6},{8,9},{9,8},{10,11... | collective-permute-start | bytes 294920 | tf_op jit(solution)/shard_map/ppermute | solution.py:407
  80.3 0.0 copy-done.2
  80.3 0.1 copy.12
  80.4 0.0 copy-done.1
  80.5 0.2 copy.11
  80.6 0.0 copy-start
  80.6 2.2 copy-done
  82.8 3.9 %turn.1 = (bf16[128,8192]{1,0:T(8,128)(2,1)}, bf16[128,8192]{1,0:T(8,128)(2,1)}) custom-call(s32[1]{0:T(128)} %bitcast.4.rep_ref, bf16[128,128,128]{2,1,0:T(8,128)(2,1)S(1)} %copy-done, bf16[128,128]{1,0:T(8,128)(2,1)S(1)} %slice_bitcast_fusion.w_ref), custom_call_target="tpu_custom_call" | custom-call | flops 536870912 | bytes 6291456 | tf_op jit(solution)/shard_map/turn/pallas_call | solution.py:129
  86.7 17.7 %collective-permute-done.other_ref = bf16[384,128]{1,0:T(8,128)(2,1)S(1)} collective-permute-done((bf16[384,128]{1,0:T(8,128)(2,1)S(1)}, bf16[384,128]{1,0:T(8,128)(2,1)S(1)}, u32[]{:S(2)}, u32[]{:S(2)}) %collective-permute-start) | collective-permute-done | bytes 98336 | tf_op jit(solution)/shard_map/ppermute | solution.py:407
  104.4 2.7 %all-to-all-done.1.hidden_ref = bf16[128,64,128]{2,1,0:T(8,128)(2,1)S(1)} async-done(((bf16[128,64,128]{2,1,0:T(8,128)(2,1)}), bf16[128,64,128]{2,1,0:T(8,128)(2,1)S(1)}, u32[]{:S(2)}, u32[]{:S(2)}) %all-to-all-start.1) | async-done | bytes 2097184 | tf_op jit(solution)/shard_map/all_to_all | solution.py:373
  107.1 7.5 %middle.1 = (bf16[128,8192]{1,0:T(8,128)(2,1)S(1)}, bf16[128,8192]{1,0:T(8,128)(2,1)S(1)}, bf16[128,2,64,128]{3,2,1,0:T(8,128)(2,1)S(1)}) custom-call(s32[1]{0:T(128)} %bitcast.4.rep_ref, bf16[128,64,128]{2,1,0:T(8,128)(2,1)S(1)} %all-to-all-done.1.hidden_ref, bf16[128,8192]{1,0:T(8,128)(2,1)} %get-tuple-element.45.state_ref, ...), custom_call_target="tpu_custom_call" | custom-call | flops 1342177280 | bytes 14680064 | tf_op jit(solution)/shard_map/middle/pallas_call | solution.py:290
  114.6 58.1 %all_to_all.21 = bf16[128,2,64,128]{3,2,1,0:T(8,128)(2,1)S(1)} all-to-all(bf16[128,2,64,128]{3,2,1,0:T(8,128)(2,1)S(1)} %get-tuple-element.50), channel_id=1, replica_groups=mesh['row'=8,'col'=8,'rep'=2] {'row','rep','col'}, dimensions={0} | all-to-all | bytes 8388608 | tf_op jit(solution)/shard_map/all_to_all | solution.py:373
  172.7 2.4 %product_in.1 = bf16[8,2,8,64,128]{4,3,2,1,0:T(8,128)(2,1)S(1)} custom-call(bf16[8,2,8,2,64,128]{5,4,3,2,1,0:T(8,128)(2,1)S(1)} %bitcast.30), custom_call_target="tpu_custom_call" | custom-call | flops 2147483648 | bytes 6291456 | tf_op jit(solution)/shard_map/product_in/pallas_call | solution.py:186
  175.0 33.8 %all_to_all.22.hidden_ref = bf16[128,64,128]{2,1,0:T(8,128)(2,1)S(1)} all-to-all(bf16[128,64,128]{2,1,0:T(8,128)(2,1)S(1)} %bitcast.31), channel_id=1, replica_groups=mesh['row'=8,'col'=8,'rep'=2] {'row','rep','col'}, dimensions={0} | all-to-all | bytes 4194304 | tf_op jit(solution)/shard_map/all_to_all | solution.py:373
  208.8 9.8 %finish.1 = bf16[128,64,128]{2,1,0:T(8,128)(2,1)} custom-call(s32[1]{0:T(128)} %bitcast.4.rep_ref, bf16[128,64,128]{2,1,0:T(8,128)(2,1)S(1)} %all_to_all.22.hidden_ref, bf16[128,8192]{1,0:T(8,128)(2,1)S(1)} %get-tuple-element.51.state_ref, bf16[128,8192]{1,0:T(8,128)(2,1)S(1)} %get-tuple-element.52.gate_ref, ...), custom_call_target="tpu_custom_call" | custom-call | flops 3489660928 | bytes 10485760 | tf_op jit(solution)/shard_map/finish/pallas_call | solution.py:353
  (9 shorter events, 0.1 us)
Async XLA Ops:
  71.0 5.9 %copy-start.7 = (bf16[2,128,128]{2,1,0:T(8,128)(2,1)S(1)}, bf16[2,128,128]{2,1,0:T(8,128)(2,1)}, u32[]{:S(2)}) copy-start(bf16[2,128,128]{2,1,0:T(8,128)(2,1)} %param.14) | copy-start | bytes 196612
  71.0 6.0 %copy-start.3 = (bf16[2,128,64]{1,2,0:T(8,128)(2,1)S(1)}, bf16[2,128,64]{1,2,0:T(8,128)(2,1)}, u32[]{:S(2)}) copy-start(bf16[2,128,64]{1,2,0:T(8,128)(2,1)} %param.10) | copy-start | bytes 98308
  71.0 6.0 %copy-start.4 = (bf16[2,128,64]{1,2,0:T(8,128)(2,1)S(1)}, bf16[2,128,64]{1,2,0:T(8,128)(2,1)}, u32[]{:S(2)}) copy-start(bf16[2,128,64]{1,2,0:T(8,128)(2,1)} %param.11) | copy-start | bytes 98308
  71.0 6.1 %copy-start.5 = (bf16[2,128,64]{1,2,0:T(8,128)(2,1)S(1)}, bf16[2,128,64]{1,2,0:T(8,128)(2,1)}, u32[]{:S(2)}) copy-start(bf16[2,128,64]{1,2,0:T(8,128)(2,1)} %param.12) | copy-start | bytes 98308
  71.0 6.1 %copy-start.6 = (bf16[2,128,64]{1,2,0:T(8,128)(2,1)S(1)}, bf16[2,128,64]{1,2,0:T(8,128)(2,1)}, u32[]{:S(2)}) copy-start(bf16[2,128,64]{1,2,0:T(8,128)(2,1)} %param.13) | copy-start | bytes 98308
  71.0 6.1 %copy-start.8 = (bf16[2,64,128]{2,1,0:T(8,128)(2,1)S(1)}, bf16[2,64,128]{2,1,0:T(8,128)(2,1)}, u32[]{:S(2)}) copy-start(bf16[2,64,128]{2,1,0:T(8,128)(2,1)} %param.15) | copy-start | bytes 98308
  71.0 9.3 %copy-start.2 = (bf16[512,128]{1,0:T(8,128)(2,1)S(1)}, bf16[512,128]{1,0:T(8,128)(2,1)}, u32[]{:S(2)}) copy-start(bf16[512,128]{1,0:T(8,128)(2,1)} %param.17) | copy-start | bytes 393220
  71.0 9.4 %copy-start.1 = (bf16[128,1024]{1,0:T(8,128)(2,1)S(1)}, bf16[128,1024]{1,0:T(8,128)(2,1)}, u32[]{:S(2)}) copy-start(bf16[128,1024]{1,0:T(8,128)(2,1)} %param.16) | copy-start | bytes 786436
  71.1 36.0 %all-to-all-start.1 = ((bf16[128,64,128]{2,1,0:T(8,128)(2,1)}), bf16[128,64,128]{2,1,0:T(8,128)(2,1)S(1)}, u32[]{:S(2)}, u32[]{:S(2)}) async-start(bf16[128,64,128]{2,1,0:T(8,128)(2,1)} %bitcast.34), calls=%async_computation.1 | async-start | bytes 4194304 | tf_op jit(solution)/shard_map/all_to_all | solution.py:373
  77.1 27.3 %collective-permute-start = (bf16[384,128]{1,0:T(8,128)(2,1)S(1)}, bf16[384,128]{1,0:T(8,128)(2,1)S(1)}, u32[]{:S(2)}, u32[]{:S(2)}) collective-permute-start(bf16[384,128]{1,0:T(8,128)(2,1)S(1)} %bitcast_dynamic-update-slice_fusion.mine_ref), channel_id=1, source_target_pairs={{0,1},{1,0},{2,3},{3,2},{4,5},{5,4},{6,7},{7,6},{8,9},{9,8},{10,11... | collective-permute-start | bytes 294920 | tf_op jit(solution)/shard_map/ppermute | solution.py:407
  80.6 2.2 %copy-start = (bf16[128,128,128]{2,1,0:T(8,128)(2,1)S(1)}, bf16[128,128,128]{2,1,0:T(8,128)(2,1)}, u32[]{:S(2)}) copy-start(bf16[128,128,128]{2,1,0:T(8,128)(2,1)} %pair_ref.2) | copy-start | bytes 12582916
